TPU v7x, 512 devices: a whole 4x4x16 slice. The times are simulated.
512 devices in a mesh: energy: 64 (over x, z), slab: 8 (over y, core).
Axes of the slice: x: 4, y: 4, z: 16, core: 2. Of those that a mesh axis runs over, the one named last changes fastest.
Arguments:
- green_block: bfloat16 [64, 8, 2, 192, 192], P('energy', 'slab'), may hold values from -0.4375 to 0.4375
- coupling: bfloat16 [64, 8, 2, 192, 192], P('energy', 'slab'), may hold values from -0.4375 to 0.4375
- sigma_lesser: bfloat16 [64, 8, 2, 192, 192], P('energy', 'slab'), may hold values from -6 to 6
- screened: bfloat16 [8, 2, 128, 36864], P('slab', None, None, 'energy'), may hold values from -9 to 9
Outputs:
- sigma_next: bfloat16 [64, 8, 2, 192, 192], P('energy', 'slab')
All inputs are finite; a program needn't handle non-finite values.
Results may differ from a plain program's by a relative error of at most 0.0049.
Values may be sent and summed in bfloat16 or wider, within the bound.
No kernel may reach another device: no remote copies, remote signals or barrier semaphores. Data moves between devices by JAX's collectives and lax.ppermute only.
A program may use at most 128 MiB of HBM per device.

v0:
```python
import math

import jax
import jax.numpy as jnp
from jax import lax
from jax.sharding import PartitionSpec as P


def from_behind(value, axis, steps):
    count = lax.axis_size(axis)
    first, last = (max(0, -steps), min(count, count - steps))
    return lax.ppermute(value, axis, [(source, source + steps) for source in range(first, last)])


def product(form, first, second):
    return jnp.einsum(form, first, second, preferred_element_type=jnp.float32)


def sandwich(outer, inner):
    outer_real = outer[:, 0]
    outer_imag = outer[:, 1]
    inner_real = inner[:, 0]
    inner_imag = inner[:, 1]
    forward = "eij,ejk->eik"
    adjoint = "eik,ejk->eij"
    half_real = (
        product(forward, outer_real, inner_real) - product(forward, outer_imag, inner_imag)
    ).astype(jnp.bfloat16)
    half_imag = (
        product(forward, outer_real, inner_imag) + product(forward, outer_imag, inner_real)
    ).astype(jnp.bfloat16)
    full_real = product(adjoint, half_real, outer_real) + product(adjoint, half_imag, outer_imag)
    full_imag = product(adjoint, half_imag, outer_real) - product(adjoint, half_real, outer_imag)
    return jnp.stack([full_real, full_imag], axis=1)


def stacked_tables(count):
    length = 2 * count
    rows = jnp.arange(length, dtype=jnp.int32)
    cols = jnp.arange(count, dtype=jnp.int32)
    phases = rows[:, None] * cols[None, :] % length
    angles = phases.astype(jnp.float32) * (2.0 * math.pi / length)
    cosine = jnp.cos(angles)
    sine = jnp.sin(angles)
    from_real = jnp.concatenate([cosine, -sine], axis=0)
    from_imag = jnp.concatenate([sine, cosine], axis=0)
    forward = jnp.stack([from_real, from_imag], axis=-1).reshape(2 * length, 2 * count)
    to_real = jnp.concatenate([cosine.T, -sine.T], axis=1)
    to_imag = jnp.concatenate([sine.T, cosine.T], axis=1)
    backward = jnp.stack([to_real, to_imag], axis=1).reshape(2 * count, 2 * length)
    return (forward, backward)


def shards(green_block, coupling, sigma_lesser, screened):
    high = lax.Precision.HIGHEST
    green_here = green_block[:, 0]
    couple_here = coupling[:, 0]
    sigma_here = sigma_lesser[:, 0]
    energies_here = green_here.shape[0]
    orbitals = green_here.shape[2]
    own_term = sandwich(green_here, sigma_here)
    couple_before = from_behind(couple_here, "slab", 1)
    made_term = sandwich(couple_before, sigma_here)
    far_term = from_behind(made_term, "slab", -1)
    lesser = (own_term + far_term).reshape(energies_here, 2, orbitals * orbitals)
    columns = lax.all_to_all(lesser, "energy", split_axis=2, concat_axis=0, tiled=True)
    total_energies = columns.shape[0]
    width = columns.shape[2]
    length = 2 * total_energies
    forward, backward = stacked_tables(total_energies)
    stacked = columns.reshape(2 * total_energies, width)
    spectrum = jnp.dot(forward, stacked, precision=high)
    spec_real = spectrum[:length]
    spec_imag = spectrum[length:]
    screen_real = screened[0, 0].astype(jnp.float32)
    screen_imag = screened[0, 1].astype(jnp.float32)
    conv_real = spec_real * screen_real - spec_imag * screen_imag
    conv_imag = spec_real * screen_imag + spec_imag * screen_real
    convolved = jnp.concatenate([conv_real, conv_imag], axis=0)
    back = jnp.dot(backward, convolved, precision=high)
    joined = (back.reshape(total_energies, 2, width) / length).astype(jnp.bfloat16)
    returned = lax.all_to_all(joined, "energy", split_axis=0, concat_axis=2, tiled=True)
    return returned.reshape(energies_here, 1, 2, orbitals, orbitals)


def solution(mesh):
    placed = (
        P("energy", "slab", None, None, None),
        P("energy", "slab", None, None, None),
        P("energy", "slab", None, None, None),
        P("slab", None, None, "energy"),
    )
    return jax.shard_map(
        shards,
        mesh=mesh,
        in_specs=placed,
        out_specs=P("energy", "slab", None, None, None),
        check_vma=False,
    )
```

profile of v0, /device:TPU:22, one launch (start us, length us, event | category | flops | bytes accessed | tf_op | source)
XLA Modules:
  0.0 324.2 jit_solution(17223660874348334574)
XLA Ops:
  0.0 1.9 collective-permute-start
  1.9 1.1 fusion.17
  3.0 1.1 fusion.19
  4.1 1.1 fusion.6
  5.3 1.1 fusion.5
  6.4 1.1 fusion.16
  7.5 0.0 collective-permute-done
  7.5 1.1 fusion.20
  8.5 1.1 fusion.21
  9.6 1.1 fusion.8
  10.7 0.2 fusion.23
  10.9 1.1 fusion.7
  11.9 0.2 fusion.22
  12.1 0.2 fusion.2
  12.4 0.2 fusion.1
  12.6 3.6 %collective-permute-start.1 = (f32[1,2,192,192]{3,2,1,0:T(8,128)S(1)}, f32[1,2,192,192]{3,2,1,0:T(8,128)S(1)}, u32[]{:S(2)}, u32[]{:S(2)}) collective-permute-start(f32[1,2,192,192]{3,2,1,0:T(8,128)S(1)} %pad_maximum_fusion), channel_id=1, source_target_pairs={{1,0},{2,1},{3,2},{4,3},{5,4},{6,5},{7,6},{9,8},{10,9},{11,10},{12... | collective-permute-start | bytes 884744 | tf_op jit(solution)/shard_map/ppermute | solution.py:12
  16.2 1.1 fusion.18
  17.3 1.1 fusion.3
  18.4 1.1 fusion.4
  19.6 2.0 collective-permute-done.1
  21.5 0.1 maximum_add_fusion
  21.6 9.7 %copy.19 = f32[1,2,192,192]{1,3,2,0:T(8,128)} copy(f32[1,2,192,192]{3,2,1,0:T(8,128)S(1)} %maximum_add_fusion) | data formatting | bytes 589824 | tf_op jit(solution)/shard_map/reshape | solution.py:65
  31.3 0.5 broadcast.37
  31.8 164.6 %reduce = f32[36864,2]{1,0:T(8,128)} reduce(f32[36864,1,2]{2,1,0:T(1,128)} %bitcast.90, f32[]{:T(128)} %broadcast.37), dimensions={1}, to_apply=%bitcast.78.reduce_sub_computation | reduce | bytes 589828
  196.4 16.0 %reshape.143 = f32[64,1,1152]{2,1,0:T(1,128)} reshape(f32[36864,2]{1,0:T(8,128)} %reduce) | data formatting | bytes 589824
  212.4 18.8 %all-to-all-start = ((f32[64,1,1152]{2,1,0:T(1,128)}), f32[64,1,1152]{2,1,0:T(1,128)S(1)}, u32[]{:S(2)}, u32[]{:S(2)}) async-start(f32[64,1,1152]{2,1,0:T(1,128)} %reshape.143), calls=%async_computation | async-start | bytes 589824 | tf_op jit(solution)/shard_map/all_to_all | solution.py:66
  231.2 0.1 fusion.41
  231.4 0.1 fusion.36
  231.6 0.1 copy.13
  231.7 0.1 pad_maximum_fusion.1
  231.8 0.1 reshape.130
  231.9 0.1 fusion.40
  232.1 0.1 fusion.38
  232.2 21.7 %all-to-all-done = f32[64,1,1152]{2,1,0:T(1,128)S(1)} async-done(((f32[64,1,1152]{2,1,0:T(1,128)}), f32[64,1,1152]{2,1,0:T(1,128)S(1)}, u32[]{:S(2)}, u32[]{:S(2)}) %all-to-all-start) | async-done | bytes 294944 | tf_op jit(solution)/shard_map/all_to_all | solution.py:66
  254.0 1.3 reduce.1
  255.3 0.0 copy-start
  255.3 30.6 %reshape.144 = f32[36864,1,2]{2,1,0:T(1,128)} reshape(f32[64,1152]{1,0:T(8,128)S(1)} %reduce.1) | data formatting | bytes 589824
  285.9 11.1 %copy.20 = f32[1,2,64,576]{3,2,1,0:T(8,128)S(1)} copy(f32[1,2,64,576]{1,3,2,0:T(8,128)} %bitcast.91) | data formatting | bytes 589824 | tf_op jit(solution)/shard_map/all_to_all | solution.py:66
  297.0 0.3 copy.16
  297.2 0.2 reshape.138
  297.5 0.7 fusion.43
  298.2 0.0 copy-done
  298.2 0.1 fusion.11
  298.3 0.7 fusion
  299.1 0.2 copy.17
  299.2 24.1 %all_to_all.30 = bf16[64,2,576]{2,1,0:T(2,128)(2,1)S(1)} all-to-all(bf16[64,2,576]{2,1,0:T(2,128)(2,1)S(1)} %copy.17), channel_id=1, replica_groups=mesh['energy'=64,'slab'=8] {'energy'}, dimensions={0} | all-to-all | bytes 294912 | tf_op jit(solution)/shard_map/all_to_all | solution.py:82
  323.4 0.9 reshape.139
  (5 shorter events, 0.1 us)
Async XLA Ops:
  0.0 7.5 %collective-permute-start = (bf16[1,2,192,192]{3,2,1,0:T(8,128)(2,1)}, bf16[1,2,192,192]{3,2,1,0:T(8,128)(2,1)S(1)}, u32[]{:S(2)}, u32[]{:S(2)}) collective-permute-start(bf16[1,2,192,192]{3,2,1,0:T(8,128)(2,1)} %bitcast.110), channel_id=1, source_target_pairs={{0,1},{1,2},{2,3},{3,4},{4,5},{5,6},{6,7},{8,9},{9,10},{10,11},{11... | collective-permute-start | bytes 442376 | tf_op jit(solution)/shard_map/ppermute | solution.py:12
  12.6 8.9 %collective-permute-start.1 = (f32[1,2,192,192]{3,2,1,0:T(8,128)S(1)}, f32[1,2,192,192]{3,2,1,0:T(8,128)S(1)}, u32[]{:S(2)}, u32[]{:S(2)}) collective-permute-start(f32[1,2,192,192]{3,2,1,0:T(8,128)S(1)} %pad_maximum_fusion), channel_id=1, source_target_pairs={{1,0},{2,1},{3,2},{4,3},{5,4},{6,5},{7,6},{9,8},{10,9},{11,10},{12... | collective-permute-start | bytes 884744 | tf_op jit(solution)/shard_map/ppermute | solution.py:12
  212.4 41.5 %all-to-all-start = ((f32[64,1,1152]{2,1,0:T(1,128)}), f32[64,1,1152]{2,1,0:T(1,128)S(1)}, u32[]{:S(2)}, u32[]{:S(2)}) async-start(f32[64,1,1152]{2,1,0:T(1,128)} %reshape.143), calls=%async_computation | async-start | bytes 589824 | tf_op jit(solution)/shard_map/all_to_all | solution.py:66
  255.3 42.9 %copy-start = (bf16[1,2,128,576]{2,3,1,0:T(8,128)(2,1)S(1)}, bf16[1,2,128,576]{2,3,1,0:T(8,128)(2,1)}, u32[]{:S(2)}) copy-start(bf16[1,2,128,576]{2,3,1,0:T(8,128)(2,1)} %param.7) | copy-start | bytes 884740
where the time goes:
time: 325 us; the launch traced here: 324 us
  other arithmetic  167 us (51%)
  local copies, waits for them, and re-layouts  69.6 us (21%)
  starting transfers between devices  24.3 us (7%)
  blocking collectives  24.1 us (7%)
  waiting for transfers between devices  23.7 us (7%)
  matrix products  15.4 us (5%)
    unnamed x1, other arithmetic  165 us
    unnamed x5, local copies, waits for them, and re-layouts  47.1 us
    all_to_all x1, blocking collectives, shards(): lax.all_to_all(joined, 'energy', split_axis=0, concat_axis=2, tiled=True)  24.1 us
    all_to_all x1, waiting for transfers between devices, shards(): lax.all_to_all(lesser, 'energy', split_axis=2, concat_axis=0, tiled=True)  21.7 us
    all_to_all x1, starting transfers between devices, shards(): lax.all_to_all(lesser, 'energy', split_axis=2, concat_axis=0, tiled=True)  18.8 us
    dot_general x16, matrix products, product(): return jnp.einsum(form, first, second, preferred_element_type=jnp.float32)  13.9 us
    all_to_all x2, local copies, waits for them, and re-layouts, shards(): lax.all_to_all(lesser, 'energy', split_axis=2, concat_axis=0, tiled=True)  11.3 us
    reshape x1, local copies, waits for them, and re-layouts, shards(): (own_term + far_term).reshape(energies_here, 2, orbitals * orbitals)  9.69 us
  transfers between devices with their start and end apart: 3, of which 2 were waited for; matrix products, arithmetic and copies ran while one was open for 3% of the time, Pallas kernels for 0%

commit v1 on v0

v1 whole, which is shorter than its diff:
```python
import math

import jax
import jax.numpy as jnp
import numpy as np
from jax import lax
from jax.experimental import pallas as pl
from jax.experimental.pallas import tpu as pltpu
from jax.sharding import PartitionSpec as P

M = 192
OWNERS = 64
ROWS = M // OWNERS
WIDTH = ROWS * M
FREQ = 128
LANES = 128


def dot(first, second):
    return jnp.dot(first, second, preferred_element_type=jnp.float32)


def dot_t(first, second):
    return lax.dot_general(first, second, (((1,), (1,)), ((), ())), preferred_element_type=jnp.float32)


def put(ref, where, value):
    for lane in range(0, value.shape[1], LANES):
        piece = value[:, lane : lane + LANES]
        ref[lane // LANES, where, : piece.shape[1]] = piece


def term(outer, inner, half, left, right):
    outer_real, outer_imag = outer[0, 0, 0], outer[0, 0, 1]
    inner_real, inner_imag = inner[0, 0, 0], inner[0, 0, 1]
    half_real = dot(outer_real, inner_real) - dot(outer_imag, inner_imag)
    half_imag = dot(outer_real, inner_imag) + dot(outer_imag, inner_real)
    put(half, slice(0, M), half_real.astype(jnp.bfloat16).astype(jnp.float32))
    put(half, slice(M, 2 * M), half_imag.astype(jnp.bfloat16).astype(jnp.float32))
    for plane in range(2):
        for row in range(ROWS):
            real = half[plane, pl.ds(row, OWNERS, stride=ROWS), :]
            imag = half[plane, pl.ds(M + row, OWNERS, stride=ROWS), :]
            first = 2 * OWNERS * row
            left[plane, pl.ds(first, OWNERS, stride=2), :] = real
            left[plane, pl.ds(first + 1, OWNERS, stride=2), :] = imag
            right[plane, pl.ds(first, OWNERS, stride=2), :] = imag
            right[plane, pl.ds(first + 1, OWNERS, stride=2), :] = -real
    left_all = jnp.concatenate([left[0], left[1, :, : M - LANES]], axis=1).astype(jnp.bfloat16)
    right_all = jnp.concatenate([right[0], right[1, :, : M - LANES]], axis=1).astype(jnp.bfloat16)
    full = dot_t(left_all, outer_real) + dot_t(right_all, outer_imag)
    return jnp.concatenate([full[2 * OWNERS * row : 2 * OWNERS * (row + 1)] for row in range(ROWS)], axis=1)


def own_kernel(green, sigma, out, half, left, right):
    out[...] = term(green, sigma, half, left, right)


def next_kernel(coupling, sigma, own, out, half, left, right):
    out[...] = (own[...] + term(coupling, sigma, half, left, right)).astype(jnp.bfloat16)


def convolve_kernel(columns, screened, forward, backward, out):
    value = columns[...]
    spectrum = dot(forward[...], jnp.concatenate([value, value], axis=0))
    spec_real, spec_imag = spectrum[:FREQ], spectrum[FREQ:]
    screen_real = screened[0, 0].astype(jnp.float32)
    screen_imag = screened[0, 1].astype(jnp.float32)
    conv_real = spec_real * screen_real - spec_imag * screen_imag
    conv_imag = spec_real * screen_imag + spec_imag * screen_real
    conv = jnp.concatenate([conv_real, conv_imag], axis=0)
    high = conv.astype(jnp.bfloat16)
    low = (conv - high.astype(jnp.float32)).astype(jnp.bfloat16)
    out[...] = dot(backward[...], jnp.concatenate([high, high, low], axis=0)).astype(jnp.bfloat16)


def unpack_kernel(packed, out, flat, rows):
    put(flat, slice(0, 2 * OWNERS), packed[...].astype(jnp.float32))
    planes = flat.shape[0]
    for part in range(2):
        both = jnp.concatenate([flat[plane, pl.ds(part, OWNERS, stride=2), :] for plane in range(planes)], axis=1)
        for row in range(ROWS):
            value = both[:, M * row : M * (row + 1)]
            put(rows, pl.ds(M * part + row, OWNERS, stride=ROWS), value)
        every = slice(M * part, M * (part + 1))
        out[0, 0, part, :, :LANES] = rows[0, every, :].astype(jnp.bfloat16)
        out[0, 0, part, :, LANES:] = rows[1, every, : M - LANES].astype(jnp.bfloat16)


def split(table):
    high = table.astype(jnp.bfloat16)
    low = (table - high.astype(np.float64)).astype(jnp.bfloat16)
    return high, low


def tables():
    phases = np.outer(np.arange(FREQ), np.arange(OWNERS)) % FREQ
    angles = phases * (2.0 * math.pi / FREQ)
    cosine, sine = np.cos(angles), np.sin(angles)
    from_real = np.concatenate([cosine, -sine], axis=0)
    from_imag = np.concatenate([sine, cosine], axis=0)
    forward = np.stack([from_real, from_imag], axis=-1).reshape(2 * FREQ, 2 * OWNERS)
    to_real = np.concatenate([cosine.T, -sine.T], axis=1)
    to_imag = np.concatenate([sine.T, cosine.T], axis=1)
    backward = np.stack([to_real, to_imag], axis=1).reshape(2 * OWNERS, 2 * FREQ) / FREQ
    forward_high, forward_low = split(forward)
    back_high, back_low = split(backward)
    return (
        np.concatenate([forward_high, forward_low], axis=1),
        np.concatenate([back_high, back_low, back_high], axis=1),
    )


def call(kernel, shape, dtype, scratch, flops, moved, *values):
    vmem = pl.BlockSpec(memory_space=pltpu.VMEM)
    return pl.pallas_call(
        kernel,
        out_shape=jax.ShapeDtypeStruct(shape, dtype),
        in_specs=[vmem] * len(values),
        out_specs=vmem,
        scratch_shapes=scratch,
        compiler_params=pltpu.CompilerParams(vmem_limit_bytes=24 * 2**20),
        cost_estimate=pl.CostEstimate(flops=flops, bytes_accessed=moved, transcendentals=0),
    )(*values)


def shards(green_block, coupling, sigma_lesser, screened):
    count = lax.axis_size("slab")
    sigma_next = lax.ppermute(sigma_lesser, "slab", [(place + 1, place) for place in range(count - 1)])
    scratch = [
        pltpu.VMEM((2, 2 * M, LANES), jnp.float32),
        pltpu.VMEM((2, 2 * M, LANES), jnp.float32),
        pltpu.VMEM((2, 2 * M, LANES), jnp.float32),
    ]
    packed = (2 * OWNERS, WIDTH)
    flops = 16 * M**3
    own = call(own_kernel, packed, jnp.float32, scratch, flops, 600000, green_block, sigma_lesser)
    lesser = call(next_kernel, packed, jnp.bfloat16, scratch, flops, 700000, coupling, sigma_next, own)
    columns = lax.all_to_all(lesser.reshape(OWNERS, 2, WIDTH), "energy", split_axis=0, concat_axis=0, tiled=True)
    forward, backward = tables()
    back = call(
        convolve_kernel, packed, jnp.bfloat16, [], 2 * 5 * 256 * 128 * WIDTH, 800000,
        columns.reshape(packed), screened, jnp.asarray(forward), jnp.asarray(backward),
    )
    returned = lax.all_to_all(back.reshape(OWNERS, 2, WIDTH), "energy", split_axis=0, concat_axis=0, tiled=True)
    return call(
        unpack_kernel, (1, 1, 2, M, M), jnp.bfloat16,
        [pltpu.VMEM((5, 2 * OWNERS, LANES), jnp.float32), pltpu.VMEM((2, 2 * M, LANES), jnp.float32)],
        1000000, 300000, returned.reshape(packed),
    )


def solution(mesh):
    placed = (
        P("energy", "slab", None, None, None),
        P("energy", "slab", None, None, None),
        P("energy", "slab", None, None, None),
        P("slab", None, None, "energy"),
    )
    return jax.shard_map(
        shards,
        mesh=mesh,
        in_specs=placed,
        out_specs=P("energy", "slab", None, None, None),
        check_vma=False,
    )
```

time: 325 us -> 69 us (0.21)
  other arithmetic: 167 us -> 0 us
  local copies, waits for them, and re-layouts: 69.6 us -> 3.15 us
  matrix products: 15.4 us -> 0 us
  waiting for transfers between devices: 23.7 us -> 18.2 us
  starting transfers between devices: 24.3 us -> 20.8 us
    unnamed x1 -> x0, other arithmetic: 165 us -> none
    unnamed x5 -> x13, local copies, waits for them, and re-layouts: 47.1 us -> 2.08 us
    dot_general x18 -> x0, matrix products: 15.4 us -> none  [the longest x16 13.9 us: product(): return jnp.einsum(form, first, second, preferred_element_type=jnp.float32)]
    all_to_all x3 -> x0, local copies, waits for them, and re-layouts: 11.3 us -> none  [the longest x2 11.3 us: shards(): lax.all_to_all(lesser, 'energy', split_axis=2, concat_axis=0, tiled=True)]
    reshape x4, local copies, waits for them, and re-layouts: 10.9 us -> 1.07 us  [the longest x1 0.74 us: shards(): lesser.reshape(OWNERS, 2, WIDTH)]
    all_to_all x1, waiting for transfers between devices: 21.7 us -> 17.2 us  [shards(): lax.all_to_all(lesser.reshape(OWNERS, 2, WIDTH), 'energy', split_axis=0,...]
    ppermute x2 -> x1, starting transfers between devices: 5.55 us -> 2.04 us  [shards(): lax.ppermute(sigma_lesser, 'slab', [(place + 1, place) for place in range...]
  transfers between devices with their start and end apart: 3 -> 2, of which waited for: 2 -> 2; matrix products, arithmetic and copies ran while one was open for 3% -> 0% of each run, Pallas kernels for 0% -> 1%
where the time goes in v1:
time: 69 us; the launch traced here: 68.8 us
  blocking collectives  23.8 us (34%)
  starting transfers between devices  20.8 us (30%)
  waiting for transfers between devices  18.2 us (26%)
  local copies, waits for them, and re-layouts  3.15 us (5%)
  Pallas kernels  2.71 us (4%)
    all_to_all x1, blocking collectives, shards(): lax.all_to_all(back.reshape(OWNERS, 2, WIDTH), 'energy', split_axis=0, co...  23.8 us
    all_to_all x1, starting transfers between devices, shards(): lax.all_to_all(lesser.reshape(OWNERS, 2, WIDTH), 'energy', split_axis=0,...  18.8 us
    all_to_all x1, waiting for transfers between devices, shards(): lax.all_to_all(lesser.reshape(OWNERS, 2, WIDTH), 'energy', split_axis=0,...  17.2 us
    pallas_call x4, Pallas kernels, call(): pl.pallas_call(kernel, out_shape=jax.ShapeDtypeStruct(shape, dtype), in_s...  2.71 us
    unnamed x13, local copies, waits for them, and re-layouts  2.08 us
    ppermute x1, starting transfers between devices, shards(): lax.ppermute(sigma_lesser, 'slab', [(place + 1, place) for place in range...  2.04 us
  transfers between devices with their start and end apart: 2, of which 2 were waited for; matrix products, arithmetic and copies ran while one was open for 0% of the time, Pallas kernels for 1%

profile of v1, /device:TPU:22, one launch (start us, length us, event | category | flops | bytes accessed | tf_op | source)
XLA Modules:
  0.0 68.8 jit_solution(17263003784480440712)
XLA Ops:
  0.0 0.0 copy-start
  0.0 2.0 %collective-permute-start = (bf16[1,1,2,192,192]{4,3,2,1,0:T(8,128)(2,1)}, bf16[1,1,2,192,192]{4,3,2,1,0:T(8,128)(2,1)S(1)}, u32[]{:S(2)}, u32[]{:S(2)}) collective-permute-start(bf16[1,1,2,192,192]{4,3,2,1,0:T(8,128)(2,1)} %sigma.1), channel_id=1, source_target_pairs={{1,0},{2,1},{3,2},{4,3},{5,4},{6,5},{7,6},{9,8},{10,9},{11,10},{12... | collective-permute-start | bytes 442376 | tf_op jit(solution)/shard_map/ppermute | solution.py:129
  2.0 0.0 copy-start.1
  2.1 0.9 %copy-done.1 = bf16[1,1,2,192,192]{4,3,2,1,0:T(8,128)(2,1)S(1)} copy-done((bf16[1,1,2,192,192]{4,3,2,1,0:T(8,128)(2,1)S(1)}, bf16[1,1,2,192,192]{4,3,2,1,0:T(8,128)(2,1)}, u32[]{:S(2)}) %copy-start.1) | copy-done | bytes 147480
  3.0 0.0 copy-start.2
  3.0 0.9 %copy-done.2 = bf16[1,1,2,192,192]{4,3,2,1,0:T(8,128)(2,1)S(1)} copy-done((bf16[1,1,2,192,192]{4,3,2,1,0:T(8,128)(2,1)S(1)}, bf16[1,1,2,192,192]{4,3,2,1,0:T(8,128)(2,1)}, u32[]{:S(2)}) %copy-start.2) | copy-done | bytes 147480
  3.9 0.6 shard_map.64.own
  4.5 1.0 %collective-permute-done.sigma = bf16[1,1,2,192,192]{4,3,2,1,0:T(8,128)(2,1)S(1)} collective-permute-done((bf16[1,1,2,192,192]{4,3,2,1,0:T(8,128)(2,1)}, bf16[1,1,2,192,192]{4,3,2,1,0:T(8,128)(2,1)S(1)}, u32[]{:S(2)}, u32[]{:S(2)}) %collective-permute-start) | collective-permute-done | bytes 147488 | tf_op jit(solution)/shard_map/ppermute | solution.py:129
  5.5 0.0 copy-done
  5.5 0.6 shard_map.65
  6.2 0.0 copy-start.5
  6.2 0.7 %reshape.12 = bf16[64,2,576]{2,1,0:T(2,128)(2,1)} reshape(bf16[128,576]{1,0:T(8,128)(2,1)S(1)} %shard_map.65) | data formatting | bytes 294912 | tf_op jit(solution)/shard_map/reshape | solution.py:139
  6.9 18.8 %all-to-all-start = ((bf16[64,2,576]{2,1,0:T(2,128)(2,1)}), bf16[64,2,576]{2,1,0:T(2,128)(2,1)S(1)}, u32[]{:S(2)}, u32[]{:S(2)}) async-start(bf16[64,2,576]{2,1,0:T(2,128)(2,1)} %reshape.12), calls=%async_computation | async-start | bytes 327680 | tf_op jit(solution)/shard_map/all_to_all | solution.py:139
  25.7 0.0 copy-done.5
  25.7 0.2 copy.8.screened
  25.9 0.0 copy-start.3
  26.0 0.0 copy-start.4
  26.0 17.2 %all-to-all-done = bf16[64,2,576]{2,1,0:T(2,128)(2,1)S(1)} async-done(((bf16[64,2,576]{2,1,0:T(2,128)(2,1)}), bf16[64,2,576]{2,1,0:T(2,128)(2,1)S(1)}, u32[]{:S(2)}, u32[]{:S(2)}) %all-to-all-start) | async-done | bytes 147488 | tf_op jit(solution)/shard_map/all_to_all | solution.py:139
  43.1 0.1 reshape.13.columns
  43.3 0.0 copy-done.3
  43.3 0.0 copy-done.4
  43.3 0.6 shard_map.66
  43.9 0.1 reshape.14
  44.0 23.8 %all_to_all.10 = bf16[64,2,576]{2,1,0:T(2,128)(2,1)S(1)} all-to-all(bf16[64,2,576]{2,1,0:T(2,128)(2,1)S(1)} %reshape.14), channel_id=1, replica_groups=mesh['energy'=64,'slab'=8] {'energy'}, dimensions={0} | all-to-all | bytes 294912 | tf_op jit(solution)/shard_map/all_to_all | solution.py:145
  67.8 0.1 reshape.15.packed
  68.0 0.8 %shard_map.67 = bf16[1,1,2,192,192]{4,3,2,1,0:T(8,128)(2,1)} custom-call(bf16[128,576]{1,0:T(8,128)(2,1)S(1)} %reshape.15.packed), custom_call_target="tpu_custom_call" | custom-call | flops 1000000 | bytes 300000 | tf_op jit(solution)/shard_map/pallas_call | solution.py:116
Async XLA Ops:
  0.0 5.5 %copy-start = (bf16[1,1,2,192,192]{4,3,2,1,0:T(8,128)(2,1)S(1)}, bf16[1,1,2,192,192]{4,3,2,1,0:T(8,128)(2,1)}, u32[]{:S(2)}) copy-start(bf16[1,1,2,192,192]{4,3,2,1,0:T(8,128)(2,1)} %coupling.1) | copy-start | bytes 442372
  0.0 5.5 %collective-permute-start = (bf16[1,1,2,192,192]{4,3,2,1,0:T(8,128)(2,1)}, bf16[1,1,2,192,192]{4,3,2,1,0:T(8,128)(2,1)S(1)}, u32[]{:S(2)}, u32[]{:S(2)}) collective-permute-start(bf16[1,1,2,192,192]{4,3,2,1,0:T(8,128)(2,1)} %sigma.1), channel_id=1, source_target_pairs={{1,0},{2,1},{3,2},{4,3},{5,4},{6,5},{7,6},{9,8},{10,9},{11,10},{12... | collective-permute-start | bytes 442376 | tf_op jit(solution)/shard_map/ppermute | solution.py:129
  2.0 0.9 %copy-start.1 = (bf16[1,1,2,192,192]{4,3,2,1,0:T(8,128)(2,1)S(1)}, bf16[1,1,2,192,192]{4,3,2,1,0:T(8,128)(2,1)}, u32[]{:S(2)}) copy-start(bf16[1,1,2,192,192]{4,3,2,1,0:T(8,128)(2,1)} %green.1) | copy-start | bytes 442372
  3.0 0.9 %copy-start.2 = (bf16[1,1,2,192,192]{4,3,2,1,0:T(8,128)(2,1)S(1)}, bf16[1,1,2,192,192]{4,3,2,1,0:T(8,128)(2,1)}, u32[]{:S(2)}) copy-start(bf16[1,1,2,192,192]{4,3,2,1,0:T(8,128)(2,1)} %sigma.1) | copy-start | bytes 442372
  6.2 19.6 %copy-start.5 = (bf16[1,2,128,576]{2,3,1,0:T(8,128)(2,1)S(1)}, bf16[1,2,128,576]{2,3,1,0:T(8,128)(2,1)}, u32[]{:S(2)}) copy-start(bf16[1,2,128,576]{2,3,1,0:T(8,128)(2,1)} %param.9) | copy-start | bytes 884740
  6.9 36.2 %all-to-all-start = ((bf16[64,2,576]{2,1,0:T(2,128)(2,1)}), bf16[64,2,576]{2,1,0:T(2,128)(2,1)S(1)}, u32[]{:S(2)}, u32[]{:S(2)}) async-start(bf16[64,2,576]{2,1,0:T(2,128)(2,1)} %reshape.12), calls=%async_computation | async-start | bytes 327680 | tf_op jit(solution)/shard_map/all_to_all | solution.py:139
  25.9 17.3 %copy-start.3 = (bf16[128,768]{1,0:T(8,128)(2,1)S(1)}, bf16[128,768]{1,0:T(8,128)(2,1)}, u32[]{:S(2)}) copy-start(bf16[128,768]{1,0:T(8,128)(2,1)} %constant.5.clone.backward) | copy-start | bytes 589828
  26.0 17.3 %copy-start.4 = (bf16[256,256]{1,0:T(8,128)(2,1)S(1)}, bf16[256,256]{1,0:T(8,128)(2,1)}, u32[]{:S(2)}) copy-start(bf16[256,256]{1,0:T(8,128)(2,1)} %constant.4.clone.forward) | copy-start | bytes 393220

commit v2 on v1

--- a/solution.py
+++ b/solution.py
@@ -57,11 +57,13 @@
 
 
 def next_kernel(coupling, sigma, own, out, half, left, right):
-    out[...] = (own[...] + term(coupling, sigma, half, left, right)).astype(jnp.bfloat16)
+    inside = lax.axis_index("slab") < lax.axis_size("slab") - 1
+    added = jnp.where(inside, term(coupling, sigma, half, left, right), 0.0)
+    out[...] = (own[...] + added).astype(jnp.bfloat16).reshape(out.shape)
 
 
 def convolve_kernel(columns, screened, forward, backward, out):
-    value = columns[...]
+    value = columns[...].reshape(2 * OWNERS, WIDTH)
     spectrum = dot(forward[...], jnp.concatenate([value, value], axis=0))
     spec_real, spec_imag = spectrum[:FREQ], spectrum[FREQ:]
     screen_real = screened[0, 0].astype(jnp.float32)
@@ -71,20 +73,24 @@
     conv = jnp.concatenate([conv_real, conv_imag], axis=0)
     high = conv.astype(jnp.bfloat16)
     low = (conv - high.astype(jnp.float32)).astype(jnp.bfloat16)
-    out[...] = dot(backward[...], jnp.concatenate([high, high, low], axis=0)).astype(jnp.bfloat16)
+    out[...] = dot(backward[...], jnp.concatenate([high, high, low], axis=0)).astype(jnp.bfloat16).reshape(out.shape)
 
 
-def unpack_kernel(packed, out, flat, rows):
-    put(flat, slice(0, 2 * OWNERS), packed[...].astype(jnp.float32))
+def unpack_kernel(packed, out, flat, rows, near, sems):
+    put(flat, slice(0, 2 * OWNERS), packed[...].reshape(2 * OWNERS, WIDTH).astype(jnp.float32))
     planes = flat.shape[0]
+    copies = [pltpu.make_async_copy(near.at[part], out.at[0, 0, part], sems.at[part]) for part in range(2)]
     for part in range(2):
         both = jnp.concatenate([flat[plane, pl.ds(part, OWNERS, stride=2), :] for plane in range(planes)], axis=1)
         for row in range(ROWS):
             value = both[:, M * row : M * (row + 1)]
             put(rows, pl.ds(M * part + row, OWNERS, stride=ROWS), value)
         every = slice(M * part, M * (part + 1))
-        out[0, 0, part, :, :LANES] = rows[0, every, :].astype(jnp.bfloat16)
-        out[0, 0, part, :, LANES:] = rows[1, every, : M - LANES].astype(jnp.bfloat16)
+        near[part, :, :LANES] = rows[0, every, :].astype(jnp.bfloat16)
+        near[part, :, LANES:] = rows[1, every, : M - LANES].astype(jnp.bfloat16)
+        copies[part].start()
+    for copy in copies:
+        copy.wait()
 
 
 def split(table):
@@ -111,13 +117,13 @@
     )
 
 
-def call(kernel, shape, dtype, scratch, flops, moved, *values):
+def call(kernel, shape, dtype, scratch, flops, moved, *values, far=False):
     vmem = pl.BlockSpec(memory_space=pltpu.VMEM)
     return pl.pallas_call(
         kernel,
         out_shape=jax.ShapeDtypeStruct(shape, dtype),
         in_specs=[vmem] * len(values),
-        out_specs=vmem,
+        out_specs=pl.BlockSpec(memory_space=pl.ANY) if far else vmem,
         scratch_shapes=scratch,
         compiler_params=pltpu.CompilerParams(vmem_limit_bytes=24 * 2**20),
         cost_estimate=pl.CostEstimate(flops=flops, bytes_accessed=moved, transcendentals=0),
@@ -126,27 +132,32 @@
 
 def shards(green_block, coupling, sigma_lesser, screened):
     count = lax.axis_size("slab")
-    sigma_next = lax.ppermute(sigma_lesser, "slab", [(place + 1, place) for place in range(count - 1)])
+    sigma_next = lax.ppermute(sigma_lesser, "slab", [((place + 1) % count, place) for place in range(count)])
     scratch = [
         pltpu.VMEM((2, 2 * M, LANES), jnp.float32),
         pltpu.VMEM((2, 2 * M, LANES), jnp.float32),
         pltpu.VMEM((2, 2 * M, LANES), jnp.float32),
     ]
-    packed = (2 * OWNERS, WIDTH)
+    packed = (OWNERS, 2, WIDTH)
     flops = 16 * M**3
-    own = call(own_kernel, packed, jnp.float32, scratch, flops, 600000, green_block, sigma_lesser)
+    own = call(own_kernel, (2 * OWNERS, WIDTH), jnp.float32, scratch, flops, 600000, green_block, sigma_lesser)
     lesser = call(next_kernel, packed, jnp.bfloat16, scratch, flops, 700000, coupling, sigma_next, own)
-    columns = lax.all_to_all(lesser.reshape(OWNERS, 2, WIDTH), "energy", split_axis=0, concat_axis=0, tiled=True)
+    columns = lax.all_to_all(lesser, "energy", split_axis=0, concat_axis=0, tiled=True)
     forward, backward = tables()
     back = call(
         convolve_kernel, packed, jnp.bfloat16, [], 2 * 5 * 256 * 128 * WIDTH, 800000,
-        columns.reshape(packed), screened, jnp.asarray(forward), jnp.asarray(backward),
+        columns, screened, jnp.asarray(forward), jnp.asarray(backward),
     )
-    returned = lax.all_to_all(back.reshape(OWNERS, 2, WIDTH), "energy", split_axis=0, concat_axis=0, tiled=True)
+    returned = lax.all_to_all(back, "energy", split_axis=0, concat_axis=0, tiled=True)
     return call(
         unpack_kernel, (1, 1, 2, M, M), jnp.bfloat16,
-        [pltpu.VMEM((5, 2 * OWNERS, LANES), jnp.float32), pltpu.VMEM((2, 2 * M, LANES), jnp.float32)],
-        1000000, 300000, returned.reshape(packed),
+        [
+            pltpu.VMEM((5, 2 * OWNERS, LANES), jnp.float32),
+            pltpu.VMEM((2, 2 * M, LANES), jnp.float32),
+            pltpu.VMEM((2, M, M), jnp.bfloat16),
+            pltpu.SemaphoreType.DMA((2,)),
+        ],
+        1000000, 300000, returned, far=True,
     )
 
 

time: 69 us -> 67.1 us (0.972)
  the two profiles are of different devices: /device:TPU:22 before, /device:TPU:24 now
where the time goes in v2:
time: 67.1 us; the launch traced here: 66.7 us
  blocking collectives  25.4 us (38%)
  starting transfers between devices  18.9 us (28%)
  waiting for transfers between devices  16.8 us (25%)
  Pallas kernels  3.51 us (5%)
  local copies, waits for them, and re-layouts  2.08 us (3%)
    all_to_all x1, blocking collectives, shards(): lax.all_to_all(back, 'energy', split_axis=0, concat_axis=0, tiled=True)  25.4 us
    all_to_all x1, starting transfers between devices, shards(): lax.all_to_all(lesser, 'energy', split_axis=0, concat_axis=0, tiled=True)  18.7 us
    all_to_all x1, waiting for transfers between devices, shards(): lax.all_to_all(lesser, 'energy', split_axis=0, concat_axis=0, tiled=True)  15.8 us
    pallas_call x4, Pallas kernels, call(): pl.pallas_call(kernel, out_shape=jax.ShapeDtypeStruct(shape, dtype), in_s...  3.51 us
    unnamed x13, local copies, waits for them, and re-layouts  2.08 us
  transfers between devices with their start and end apart: 2, of which 2 were waited for; matrix products, arithmetic and copies ran while one was open for 0% of the time, Pallas kernels for 1%

profile of v2, /device:TPU:24, one launch (start us, length us, event | category | flops | bytes accessed | tf_op | source)
XLA Modules:
  0.0 66.7 jit_solution(3472930415525461239)
XLA Ops:
  0.0 0.0 copy-start
  0.0 0.2 collective-permute-start
  0.2 0.0 copy-start.1
  0.2 0.9 %copy-done.1 = bf16[1,1,2,192,192]{4,3,2,1,0:T(8,128)(2,1)S(1)} copy-done((bf16[1,1,2,192,192]{4,3,2,1,0:T(8,128)(2,1)S(1)}, bf16[1,1,2,192,192]{4,3,2,1,0:T(8,128)(2,1)}, u32[]{:S(2)}) %copy-start.1) | copy-done | bytes 147480
  1.1 0.0 copy-start.2
  1.1 0.9 %copy-done.2 = bf16[1,1,2,192,192]{4,3,2,1,0:T(8,128)(2,1)S(1)} copy-done((bf16[1,1,2,192,192]{4,3,2,1,0:T(8,128)(2,1)S(1)}, bf16[1,1,2,192,192]{4,3,2,1,0:T(8,128)(2,1)}, u32[]{:S(2)}) %copy-start.2) | copy-done | bytes 147480
  2.0 0.6 shard_map.64.own
  2.7 1.0 %collective-permute-done.sigma = bf16[1,1,2,192,192]{4,3,2,1,0:T(8,128)(2,1)S(1)} collective-permute-done((bf16[1,1,2,192,192]{4,3,2,1,0:T(8,128)(2,1)}, bf16[1,1,2,192,192]{4,3,2,1,0:T(8,128)(2,1)S(1)}, u32[]{:S(2)}, u32[]{:S(2)}) %collective-permute-start) | collective-permute-done | bytes 147488 | tf_op jit(solution)/shard_map/ppermute | solution.py:135
  3.7 0.0 copy-done
  3.7 1.3 %shard_map.65 = bf16[64,2,576]{2,1,0:T(2,128)(2,1)} custom-call(bf16[1,1,2,192,192]{4,3,2,1,0:T(8,128)(2,1)S(1)} %copy-done, bf16[1,1,2,192,192]{4,3,2,1,0:T(8,128)(2,1)S(1)} %collective-permute-done.sigma, f32[128,576]{1,0:T(8,128)S(1)} %shard_map.64.own), custom_call_target="tpu_custom_call" | custom-call | flops 113246208 | bytes 700000 | tf_op jit(solution)/shard_map/pallas_call | solution.py:122
  5.0 0.0 copy-start.5
  5.0 18.7 %all-to-all-start = ((bf16[64,2,576]{2,1,0:T(2,128)(2,1)}), bf16[64,2,576]{2,1,0:T(2,128)(2,1)S(1)}, u32[]{:S(2)}, u32[]{:S(2)}) async-start(bf16[64,2,576]{2,1,0:T(2,128)(2,1)} %shard_map.65), calls=%async_computation | async-start | bytes 327680 | tf_op jit(solution)/shard_map/all_to_all | solution.py:145
  23.7 0.0 copy-done.5
  23.7 0.0 copy-start.3
  23.7 0.0 copy-start.4
  23.7 0.2 copy.7.screened
  24.0 15.8 %all-to-all-done.columns = bf16[64,2,576]{2,1,0:T(2,128)(2,1)S(1)} async-done(((bf16[64,2,576]{2,1,0:T(2,128)(2,1)}), bf16[64,2,576]{2,1,0:T(2,128)(2,1)S(1)}, u32[]{:S(2)}, u32[]{:S(2)}) %all-to-all-start) | async-done | bytes 147488 | tf_op jit(solution)/shard_map/all_to_all | solution.py:145
  39.8 0.0 copy-done.3
  39.8 0.0 copy-done.4
  39.8 0.6 shard_map.66
  40.5 25.4 %all_to_all.10.packed = bf16[64,2,576]{2,1,0:T(2,128)(2,1)S(1)} all-to-all(bf16[64,2,576]{2,1,0:T(2,128)(2,1)S(1)} %shard_map.66), channel_id=1, replica_groups=mesh['energy'=64,'slab'=8] {'energy'}, dimensions={0} | all-to-all | bytes 294912 | tf_op jit(solution)/shard_map/all_to_all | solution.py:151
  65.8 0.9 %shard_map.67 = bf16[1,1,2,192,192]{4,3,2,1,0:T(8,128)(2,1)} custom-call(bf16[64,2,576]{2,1,0:T(2,128)(2,1)S(1)} %all_to_all.10.packed), custom_call_target="tpu_custom_call" | custom-call | flops 1000000 | bytes 300000 | tf_op jit(solution)/shard_map/pallas_call | solution.py:122
Async XLA Ops:
  0.0 3.7 %copy-start = (bf16[1,1,2,192,192]{4,3,2,1,0:T(8,128)(2,1)S(1)}, bf16[1,1,2,192,192]{4,3,2,1,0:T(8,128)(2,1)}, u32[]{:S(2)}) copy-start(bf16[1,1,2,192,192]{4,3,2,1,0:T(8,128)(2,1)} %coupling.1) | copy-start | bytes 442372
  0.0 3.7 %collective-permute-start = (bf16[1,1,2,192,192]{4,3,2,1,0:T(8,128)(2,1)}, bf16[1,1,2,192,192]{4,3,2,1,0:T(8,128)(2,1)S(1)}, u32[]{:S(2)}, u32[]{:S(2)}) collective-permute-start(bf16[1,1,2,192,192]{4,3,2,1,0:T(8,128)(2,1)} %sigma.1), channel_id=1, source_target_pairs={{1,0},{2,1},{3,2},{4,3},{5,4},{6,5},{7,6},{0,7},{9,8},{10,9},{11,1... | collective-permute-start | bytes 442376 | tf_op jit(solution)/shard_map/ppermute | solution.py:135
  0.2 0.9 %copy-start.1 = (bf16[1,1,2,192,192]{4,3,2,1,0:T(8,128)(2,1)S(1)}, bf16[1,1,2,192,192]{4,3,2,1,0:T(8,128)(2,1)}, u32[]{:S(2)}) copy-start(bf16[1,1,2,192,192]{4,3,2,1,0:T(8,128)(2,1)} %green.1) | copy-start | bytes 442372
  1.1 0.9 %copy-start.2 = (bf16[1,1,2,192,192]{4,3,2,1,0:T(8,128)(2,1)S(1)}, bf16[1,1,2,192,192]{4,3,2,1,0:T(8,128)(2,1)}, u32[]{:S(2)}) copy-start(bf16[1,1,2,192,192]{4,3,2,1,0:T(8,128)(2,1)} %sigma.1) | copy-start | bytes 442372
  5.0 18.7 %copy-start.5 = (bf16[1,2,128,576]{2,3,1,0:T(8,128)(2,1)S(1)}, bf16[1,2,128,576]{2,3,1,0:T(8,128)(2,1)}, u32[]{:S(2)}) copy-start(bf16[1,2,128,576]{2,3,1,0:T(8,128)(2,1)} %param.9) | copy-start | bytes 884740
  5.0 34.8 %all-to-all-start = ((bf16[64,2,576]{2,1,0:T(2,128)(2,1)}), bf16[64,2,576]{2,1,0:T(2,128)(2,1)S(1)}, u32[]{:S(2)}, u32[]{:S(2)}) async-start(bf16[64,2,576]{2,1,0:T(2,128)(2,1)} %shard_map.65), calls=%async_computation | async-start | bytes 327680 | tf_op jit(solution)/shard_map/all_to_all | solution.py:145
  23.7 16.1 %copy-start.3 = (bf16[128,768]{1,0:T(8,128)(2,1)S(1)}, bf16[128,768]{1,0:T(8,128)(2,1)}, u32[]{:S(2)}) copy-start(bf16[128,768]{1,0:T(8,128)(2,1)} %constant.5.clone.backward) | copy-start | bytes 589828
  23.7 16.1 %copy-start.4 = (bf16[256,256]{1,0:T(8,128)(2,1)S(1)}, bf16[256,256]{1,0:T(8,128)(2,1)}, u32[]{:S(2)}) copy-start(bf16[256,256]{1,0:T(8,128)(2,1)} %constant.4.clone.forward) | copy-start | bytes 393220

commit v3 on v2

--- a/solution.py
+++ b/solution.py
@@ -62,12 +62,19 @@
     out[...] = (own[...] + added).astype(jnp.bfloat16).reshape(out.shape)
 
 
+def prepare_kernel(screened, forward, backward, turned, forward_out, backward_out):
+    for part in range(2):
+        turned[part] = screened[0, part].T
+    forward_out[...] = forward[...]
+    backward_out[...] = backward[...]
+
+
 def convolve_kernel(columns, screened, forward, backward, out):
     value = columns[...].reshape(2 * OWNERS, WIDTH)
     spectrum = dot(forward[...], jnp.concatenate([value, value], axis=0))
     spec_real, spec_imag = spectrum[:FREQ], spectrum[FREQ:]
-    screen_real = screened[0, 0].astype(jnp.float32)
-    screen_imag = screened[0, 1].astype(jnp.float32)
+    screen_real = screened[0].astype(jnp.float32)
+    screen_imag = screened[1].astype(jnp.float32)
     conv_real = spec_real * screen_real - spec_imag * screen_imag
     conv_imag = spec_real * screen_imag + spec_imag * screen_real
     conv = jnp.concatenate([conv_real, conv_imag], axis=0)
@@ -117,13 +124,17 @@
     )
 
 
-def call(kernel, shape, dtype, scratch, flops, moved, *values, far=False):
+def shaped(shape, dtype=jnp.bfloat16):
+    return jax.ShapeDtypeStruct(shape, dtype)
+
+
+def call(kernel, shapes, flops, moved, *values, scratch=(), far=False):
     vmem = pl.BlockSpec(memory_space=pltpu.VMEM)
     return pl.pallas_call(
         kernel,
-        out_shape=jax.ShapeDtypeStruct(shape, dtype),
+        out_shape=shapes,
         in_specs=[vmem] * len(values),
-        out_specs=pl.BlockSpec(memory_space=pl.ANY) if far else vmem,
+        out_specs=[pl.BlockSpec(memory_space=pl.ANY) if far else vmem] * len(shapes),
         scratch_shapes=scratch,
         compiler_params=pltpu.CompilerParams(vmem_limit_bytes=24 * 2**20),
         cost_estimate=pl.CostEstimate(flops=flops, bytes_accessed=moved, transcendentals=0),
@@ -133,32 +144,31 @@
 def shards(green_block, coupling, sigma_lesser, screened):
     count = lax.axis_size("slab")
     sigma_next = lax.ppermute(sigma_lesser, "slab", [((place + 1) % count, place) for place in range(count)])
-    scratch = [
-        pltpu.VMEM((2, 2 * M, LANES), jnp.float32),
-        pltpu.VMEM((2, 2 * M, LANES), jnp.float32),
-        pltpu.VMEM((2, 2 * M, LANES), jnp.float32),
-    ]
-    packed = (OWNERS, 2, WIDTH)
+    planes = [pltpu.VMEM((2, 2 * M, LANES), jnp.float32)] * 3
+    packed = shaped((OWNERS, 2, WIDTH))
     flops = 16 * M**3
-    own = call(own_kernel, (2 * OWNERS, WIDTH), jnp.float32, scratch, flops, 600000, green_block, sigma_lesser)
-    lesser = call(next_kernel, packed, jnp.bfloat16, scratch, flops, 700000, coupling, sigma_next, own)
+    (own,) = call(own_kernel, [shaped((2 * OWNERS, WIDTH), jnp.float32)], flops, 600000, green_block, sigma_lesser, scratch=planes)
+    forward, backward = tables()
+    turned, forward, backward = call(
+        prepare_kernel, [shaped((2, FREQ, WIDTH)), shaped(forward.shape), shaped(backward.shape)], flops, 1200000,
+        screened.transpose(0, 1, 3, 2), jnp.asarray(forward), jnp.asarray(backward),
+    )
+    own, turned, forward, backward = lax.optimization_barrier((own, turned, forward, backward))
+    (lesser,) = call(next_kernel, [packed], flops, 700000, coupling, sigma_next, own, scratch=planes)
     columns = lax.all_to_all(lesser, "energy", split_axis=0, concat_axis=0, tiled=True)
-    forward, backward = tables()
-    back = call(
-        convolve_kernel, packed, jnp.bfloat16, [], 2 * 5 * 256 * 128 * WIDTH, 800000,
-        columns, screened, jnp.asarray(forward), jnp.asarray(backward),
-    )
-    returned = lax.all_to_all(back, "energy", split_axis=0, concat_axis=0, tiled=True)
-    return call(
-        unpack_kernel, (1, 1, 2, M, M), jnp.bfloat16,
-        [
+    (joined,) = call(convolve_kernel, [packed], 2 * 5 * 256 * 128 * WIDTH, 800000, columns, turned, forward, backward)
+    returned = lax.all_to_all(joined, "energy", split_axis=0, concat_axis=0, tiled=True)
+    (result,) = call(
+        unpack_kernel, [shaped(sigma_lesser.shape)], 1000000, 300000, returned,
+        scratch=[
             pltpu.VMEM((5, 2 * OWNERS, LANES), jnp.float32),
             pltpu.VMEM((2, 2 * M, LANES), jnp.float32),
             pltpu.VMEM((2, M, M), jnp.bfloat16),
             pltpu.SemaphoreType.DMA((2,)),
         ],
-        1000000, 300000, returned, far=True,
+        far=True,
     )
+    return result
 
 
 def solution(mesh):

time: 67.1 us -> 66.2 us (0.987)
  blocking collectives: 25.4 us -> 59.8 us
  starting transfers between devices: 18.9 us -> 0.18 us
  waiting for transfers between devices: 16.8 us -> 0.6 us
    all_to_all x1 -> x2, blocking collectives: 25.4 us -> 59.8 us  [the longest x1 34.7 us: shards(): lax.all_to_all(lesser, 'energy', split_axis=0, concat_axis=0, tiled=True)]
    all_to_all x1 -> x0, starting transfers between devices: 18.7 us -> none  [shards(): lax.all_to_all(lesser, 'energy', split_axis=0, concat_axis=0, tiled=True)]
    all_to_all x1 -> x0, waiting for transfers between devices: 15.8 us -> none  [shards(): lax.all_to_all(lesser, 'energy', split_axis=0, concat_axis=0, tiled=True)]
    pallas_call x4 -> x5, Pallas kernels: 3.51 us -> 2.97 us  [call(): pl.pallas_call(kernel, out_shape=shapes, in_specs=[vmem] * len(values), o...]
    unnamed x13 -> x12, local copies, waits for them, and re-layouts: 2.08 us -> 2.29 us
  transfers between devices with their start and end apart: 2 -> 1, of which waited for: 2 -> 1; matrix products, arithmetic and copies ran while one was open for 0% -> 0% of each run, Pallas kernels for 1% -> 1%
where the time goes in v3:
time: 66.2 us; the launch traced here: 65.9 us
  blocking collectives  59.8 us (90%)
  Pallas kernels  2.97 us (4%)
  local copies, waits for them, and re-layouts  2.29 us (3%)
    all_to_all x1, blocking collectives, shards(): lax.all_to_all(lesser, 'energy', split_axis=0, concat_axis=0, tiled=True)  34.7 us
    all_to_all x1, blocking collectives, shards(): lax.all_to_all(joined, 'energy', split_axis=0, concat_axis=0, tiled=True)  25.1 us
    pallas_call x5, Pallas kernels, call(): pl.pallas_call(kernel, out_shape=shapes, in_specs=[vmem] * len(values), o...  2.97 us
    unnamed x12, local copies, waits for them, and re-layouts  2.29 us
  transfers between devices with their start and end apart: 1, of which 1 were waited for; matrix products, arithmetic and copies ran while one was open for 0% of the time, Pallas kernels for 1%

profile of v3, /device:TPU:24, one launch (start us, length us, event | category | flops | bytes accessed | tf_op | source)
XLA Modules:
  0.0 65.9 jit_solution(9259412090574284031)
XLA Ops:
  0.0 0.0 copy-start.2
  0.0 0.0 copy-start
  0.0 0.2 collective-permute-start
  0.2 0.0 copy-start.3
  0.2 0.9 %copy-done.3 = bf16[1,1,2,192,192]{4,3,2,1,0:T(8,128)(2,1)S(1)} copy-done((bf16[1,1,2,192,192]{4,3,2,1,0:T(8,128)(2,1)S(1)}, bf16[1,1,2,192,192]{4,3,2,1,0:T(8,128)(2,1)}, u32[]{:S(2)}) %copy-start.3) | copy-done | bytes 147480
  1.1 0.0 copy-start.4
  1.1 0.9 %copy-done.4 = bf16[1,1,2,192,192]{4,3,2,1,0:T(8,128)(2,1)S(1)} copy-done((bf16[1,1,2,192,192]{4,3,2,1,0:T(8,128)(2,1)S(1)}, bf16[1,1,2,192,192]{4,3,2,1,0:T(8,128)(2,1)}, u32[]{:S(2)}) %copy-start.4) | copy-done | bytes 147480
  2.0 0.0 copy-start.5
  2.0 0.6 shard_map.64.own
  2.7 0.0 copy-done.2
  2.7 0.0 copy-done
  2.7 0.2 copy-done.5
  2.9 0.0 copy-start.1
  2.9 0.1 shard_map.65
  3.1 0.6 collective-permute-done.sigma
  3.7 0.2 copy-done.1
  3.9 0.6 shard_map.66
  4.5 34.7 %all_to_all.10.columns = bf16[64,2,576]{2,1,0:T(2,128)(2,1)S(1)} all-to-all(bf16[64,2,576]{2,1,0:T(2,128)(2,1)S(1)} %shard_map.66), channel_id=1, replica_groups=mesh['energy'=64,'slab'=8] {'energy'}, dimensions={0} | all-to-all | bytes 294912 | tf_op jit(solution)/shard_map/all_to_all | solution.py:158
  39.3 0.6 shard_map.67
  39.9 25.1 %all_to_all.11.packed = bf16[64,2,576]{2,1,0:T(2,128)(2,1)S(1)} all-to-all(bf16[64,2,576]{2,1,0:T(2,128)(2,1)S(1)} %shard_map.67), channel_id=1, replica_groups=mesh['energy'=64,'slab'=8] {'energy'}, dimensions={0} | all-to-all | bytes 294912 | tf_op jit(solution)/shard_map/all_to_all | solution.py:160
  65.0 0.9 %shard_map.68 = bf16[1,1,2,192,192]{4,3,2,1,0:T(8,128)(2,1)} custom-call(bf16[64,2,576]{2,1,0:T(2,128)(2,1)S(1)} %all_to_all.11.packed), custom_call_target="tpu_custom_call" | custom-call | flops 1000000 | bytes 300000 | tf_op jit(solution)/shard_map/pallas_call | solution.py:133
Async XLA Ops:
  0.0 2.7 %copy-start.2 = (bf16[128,768]{1,0:T(8,128)(2,1)S(1)}, bf16[128,768]{1,0:T(8,128)(2,1)}, u32[]{:S(2)}) copy-start(bf16[128,768]{1,0:T(8,128)(2,1)} %constant.5.clone.backward) | copy-start | bytes 589828
  0.0 2.7 %copy-start = (bf16[1,2,128,576]{2,3,1,0:T(8,128)(2,1)S(1)}, bf16[1,2,128,576]{2,3,1,0:T(8,128)(2,1)}, u32[]{:S(2)}) copy-start(bf16[1,2,128,576]{2,3,1,0:T(8,128)(2,1)} %param.9) | copy-start | bytes 884740
  0.0 3.7 %collective-permute-start = (bf16[1,1,2,192,192]{4,3,2,1,0:T(8,128)(2,1)}, bf16[1,1,2,192,192]{4,3,2,1,0:T(8,128)(2,1)S(1)}, u32[]{:S(2)}, u32[]{:S(2)}) collective-permute-start(bf16[1,1,2,192,192]{4,3,2,1,0:T(8,128)(2,1)} %sigma.1), channel_id=1, source_target_pairs={{1,0},{2,1},{3,2},{4,3},{5,4},{6,5},{7,6},{0,7},{9,8},{10,9},{11,1... | collective-permute-start | bytes 442376 | tf_op jit(solution)/shard_map/ppermute | solution.py:146
  0.2 0.9 %copy-start.3 = (bf16[1,1,2,192,192]{4,3,2,1,0:T(8,128)(2,1)S(1)}, bf16[1,1,2,192,192]{4,3,2,1,0:T(8,128)(2,1)}, u32[]{:S(2)}) copy-start(bf16[1,1,2,192,192]{4,3,2,1,0:T(8,128)(2,1)} %green.1) | copy-start | bytes 442372
  1.1 0.9 %copy-start.4 = (bf16[1,1,2,192,192]{4,3,2,1,0:T(8,128)(2,1)S(1)}, bf16[1,1,2,192,192]{4,3,2,1,0:T(8,128)(2,1)}, u32[]{:S(2)}) copy-start(bf16[1,1,2,192,192]{4,3,2,1,0:T(8,128)(2,1)} %sigma.1) | copy-start | bytes 442372
  2.0 0.9 %copy-start.5 = (bf16[256,256]{1,0:T(8,128)(2,1)S(1)}, bf16[256,256]{1,0:T(8,128)(2,1)}, u32[]{:S(2)}) copy-start(bf16[256,256]{1,0:T(8,128)(2,1)} %constant.4.clone.forward) | copy-start | bytes 393220
  2.9 0.9 %copy-start.1 = (bf16[1,1,2,192,192]{4,3,2,1,0:T(8,128)(2,1)S(1)}, bf16[1,1,2,192,192]{4,3,2,1,0:T(8,128)(2,1)}, u32[]{:S(2)}) copy-start(bf16[1,1,2,192,192]{4,3,2,1,0:T(8,128)(2,1)} %coupling.1) | copy-start | bytes 442372

commit v4 on v3

--- a/solution.py
+++ b/solution.py
@@ -14,6 +14,18 @@
 WIDTH = ROWS * M
 FREQ = 128
 LANES = 128
+FIRST = [
+    10, 20, 12, 31, 50, 55, 19, 56, 43, 45, 0, 21, 1, 16, 8, 22,
+    11, 54, 53, 42, 24, 29, 18, 33, 30, 28, 49, 61, 44, 40, 17, 48,
+    38, 59, 62, 39, 14, 7, 36, 51, 46, 35, 47, 15, 57, 26, 27, 5,
+    2, 13, 32, 58, 37, 23, 6, 34, 52, 4, 3, 63, 25, 9, 60, 41,
+]
+SECOND = [
+    10, 20, 12, 31, 50, 55, 19, 56, 43, 45, 0, 21, 1, 16, 8, 22,
+    11, 54, 53, 42, 24, 29, 18, 33, 30, 28, 49, 61, 44, 40, 17, 48,
+    38, 59, 62, 39, 14, 7, 36, 51, 46, 35, 47, 15, 57, 26, 27, 5,
+    2, 13, 32, 58, 37, 23, 6, 34, 52, 4, 3, 63, 25, 9, 60, 41,
+]
 
 
 def dot(first, second):
@@ -59,7 +71,9 @@
 def next_kernel(coupling, sigma, own, out, half, left, right):
     inside = lax.axis_index("slab") < lax.axis_size("slab") - 1
     added = jnp.where(inside, term(coupling, sigma, half, left, right), 0.0)
-    out[...] = (own[...] + added).astype(jnp.bfloat16).reshape(out.shape)
+    chunks = (own[...] + added).astype(jnp.bfloat16).reshape(out.shape)
+    for place, owner in enumerate(FIRST):
+        out[place] = chunks[owner]
 
 
 def prepare_kernel(screened, forward, backward, turned, forward_out, backward_out):
@@ -84,7 +98,9 @@
 
 
 def unpack_kernel(packed, out, flat, rows, near, sems):
-    put(flat, slice(0, 2 * OWNERS), packed[...].reshape(2 * OWNERS, WIDTH).astype(jnp.float32))
+    places = [SECOND.index(owner) for owner in range(OWNERS)]
+    value = jnp.concatenate([packed[place : place + 1] for place in places], axis=0).reshape(2 * OWNERS, WIDTH)
+    put(flat, slice(0, 2 * OWNERS), value.astype(jnp.float32))
     planes = flat.shape[0]
     copies = [pltpu.make_async_copy(near.at[part], out.at[0, 0, part], sems.at[part]) for part in range(2)]
     for part in range(2):
@@ -112,10 +128,10 @@
     cosine, sine = np.cos(angles), np.sin(angles)
     from_real = np.concatenate([cosine, -sine], axis=0)
     from_imag = np.concatenate([sine, cosine], axis=0)
-    forward = np.stack([from_real, from_imag], axis=-1).reshape(2 * FREQ, 2 * OWNERS)
+    forward = np.stack([from_real, from_imag], axis=-1)[:, FIRST].reshape(2 * FREQ, 2 * OWNERS)
     to_real = np.concatenate([cosine.T, -sine.T], axis=1)
     to_imag = np.concatenate([sine.T, cosine.T], axis=1)
-    backward = np.stack([to_real, to_imag], axis=1).reshape(2 * OWNERS, 2 * FREQ) / FREQ
+    backward = np.stack([to_real, to_imag], axis=1)[SECOND].reshape(2 * OWNERS, 2 * FREQ) / FREQ
     forward_high, forward_low = split(forward)
     back_high, back_low = split(backward)
     return (
@@ -155,9 +171,9 @@
     )
     own, turned, forward, backward = lax.optimization_barrier((own, turned, forward, backward))
     (lesser,) = call(next_kernel, [packed], flops, 700000, coupling, sigma_next, own, scratch=planes)
-    columns = lax.all_to_all(lesser, "energy", split_axis=0, concat_axis=0, tiled=True)
+    columns = lax.all_to_all(lesser, "energy", split_axis=0, concat_axis=0, axis_index_groups=[FIRST], tiled=True)
     (joined,) = call(convolve_kernel, [packed], 2 * 5 * 256 * 128 * WIDTH, 800000, columns, turned, forward, backward)
-    returned = lax.all_to_all(joined, "energy", split_axis=0, concat_axis=0, tiled=True)
+    returned = lax.all_to_all(joined, "energy", split_axis=0, concat_axis=0, axis_index_groups=[SECOND], tiled=True)
     (result,) = call(
         unpack_kernel, [shaped(sigma_lesser.shape)], 1000000, 300000, returned,
         scratch=[

time: 66.2 us -> 62.6 us (0.946)
  blocking collectives: 59.8 us -> 56.2 us
    all_to_all x2, blocking collectives: 59.8 us -> 56.2 us  [the longest x1 32.1 us: shards(): lax.all_to_all(lesser, 'energy', split_axis=0, concat_axis=0, axis_index_...]
where the time goes in v4:
time: 62.6 us; the launch traced here: 62.3 us
  blocking collectives  56.2 us (90%)
  Pallas kernels  2.98 us (5%)
  local copies, waits for them, and re-layouts  2.29 us (4%)
    all_to_all x1, blocking collectives, shards(): lax.all_to_all(lesser, 'energy', split_axis=0, concat_axis=0, axis_index_...  32.1 us
    all_to_all x1, blocking collectives, shards(): lax.all_to_all(joined, 'energy', split_axis=0, concat_axis=0, axis_index_...  24.1 us
    pallas_call x5, Pallas kernels, call(): pl.pallas_call(kernel, out_shape=shapes, in_specs=[vmem] * len(values), o...  2.98 us
    unnamed x12, local copies, waits for them, and re-layouts  2.29 us
  transfers between devices with their start and end apart: 1, of which 1 were waited for; matrix products, arithmetic and copies ran while one was open for 0% of the time, Pallas kernels for 1%

profile of v4, /device:TPU:24, one launch (start us, length us, event | category | flops | bytes accessed | tf_op | source)
XLA Modules:
  0.0 62.3 jit_solution(16069172396080862301)
XLA Ops:
  0.0 0.0 copy-start.2
  0.0 0.0 copy-start
  0.0 0.2 collective-permute-start
  0.2 0.0 copy-start.3
  0.2 0.9 %copy-done.3 = bf16[1,1,2,192,192]{4,3,2,1,0:T(8,128)(2,1)S(1)} copy-done((bf16[1,1,2,192,192]{4,3,2,1,0:T(8,128)(2,1)S(1)}, bf16[1,1,2,192,192]{4,3,2,1,0:T(8,128)(2,1)}, u32[]{:S(2)}) %copy-start.3) | copy-done | bytes 147480
  1.1 0.0 copy-start.4
  1.1 0.9 %copy-done.4 = bf16[1,1,2,192,192]{4,3,2,1,0:T(8,128)(2,1)S(1)} copy-done((bf16[1,1,2,192,192]{4,3,2,1,0:T(8,128)(2,1)S(1)}, bf16[1,1,2,192,192]{4,3,2,1,0:T(8,128)(2,1)}, u32[]{:S(2)}) %copy-start.4) | copy-done | bytes 147480
  2.0 0.0 copy-start.5
  2.0 0.6 %shard_map.64.own = f32[128,576]{1,0:T(8,128)S(1)} custom-call(bf16[1,1,2,192,192]{4,3,2,1,0:T(8,128)(2,1)S(1)} %copy-done.3, bf16[1,1,2,192,192]{4,3,2,1,0:T(8,128)(2,1)S(1)} %copy-done.4), custom_call_target="tpu_custom_call" | custom-call | flops 113246208 | bytes 600000 | tf_op jit(solution)/shard_map/pallas_call | solution.py:149
  2.7 0.0 copy-done.2
  2.7 0.0 copy-done
  2.7 0.2 copy-done.5
  2.9 0.0 copy-start.1
  2.9 0.1 shard_map.65
  3.1 0.6 collective-permute-done.sigma
  3.7 0.2 copy-done.1
  3.9 0.6 %shard_map.66 = bf16[64,2,576]{2,1,0:T(2,128)(2,1)S(1)} custom-call(bf16[1,1,2,192,192]{4,3,2,1,0:T(8,128)(2,1)S(1)} %copy-done.1, bf16[1,1,2,192,192]{4,3,2,1,0:T(8,128)(2,1)S(1)} %collective-permute-done.sigma, f32[128,576]{1,0:T(8,128)S(1)} %shard_map.64.own), custom_call_target="tpu_custom_call" | custom-call | flops 113246208 | bytes 700000 | tf_op jit(solution)/shard_map/pallas_call | solution.py:149
  4.5 32.1 %all_to_all.10.columns = bf16[64,2,576]{2,1,0:T(2,128)(2,1)S(1)} all-to-all(bf16[64,2,576]{2,1,0:T(2,128)(2,1)S(1)} %shard_map.66), channel_id=1, replica_groups={{80,160,96,248,400,440,152,448,344,360,0,168,8,128,64,176,88,432,424,33..., dimensions={0} | all-to-all | bytes 294912 | tf_op jit(solution)/shard_map/all_to_all | solution.py:174
  36.6 0.6 %shard_map.67 = bf16[64,2,576]{2,1,0:T(2,128)(2,1)S(1)} custom-call(bf16[64,2,576]{2,1,0:T(2,128)(2,1)S(1)} %all_to_all.10.columns, bf16[2,128,576]{2,1,0:T(8,128)(2,1)S(1)} %get-tuple-element.16.screened, bf16[256,256]{1,0:T(8,128)(2,1)S(1)} %get-tuple-element.17.forward, bf16[128,768]{1,0:T(8,128)(2,1)S(1)} %get-tuple-element.18.backward), custom_call_target="tpu_custom_call" | custom-call | flops 188743680 | bytes 800000 | tf_op jit(solution)/shard_map/pallas_call | solution.py:149
  37.3 24.1 %all_to_all.11.packed = bf16[64,2,576]{2,1,0:T(2,128)(2,1)S(1)} all-to-all(bf16[64,2,576]{2,1,0:T(2,128)(2,1)S(1)} %shard_map.67), channel_id=1, replica_groups={{80,160,96,248,400,440,152,448,344,360,0,168,8,128,64,176,88,432,424,33..., dimensions={0} | all-to-all | bytes 294912 | tf_op jit(solution)/shard_map/all_to_all | solution.py:176
  61.4 0.9 %shard_map.68 = bf16[1,1,2,192,192]{4,3,2,1,0:T(8,128)(2,1)} custom-call(bf16[64,2,576]{2,1,0:T(2,128)(2,1)S(1)} %all_to_all.11.packed), custom_call_target="tpu_custom_call" | custom-call | flops 1000000 | bytes 300000 | tf_op jit(solution)/shard_map/pallas_call | solution.py:149
Async XLA Ops:
  0.0 2.7 %copy-start.2 = (bf16[128,768]{1,0:T(8,128)(2,1)S(1)}, bf16[128,768]{1,0:T(8,128)(2,1)}, u32[]{:S(2)}) copy-start(bf16[128,768]{1,0:T(8,128)(2,1)} %constant.5.clone.backward) | copy-start | bytes 589828
  0.0 2.7 %copy-start = (bf16[1,2,128,576]{2,3,1,0:T(8,128)(2,1)S(1)}, bf16[1,2,128,576]{2,3,1,0:T(8,128)(2,1)}, u32[]{:S(2)}) copy-start(bf16[1,2,128,576]{2,3,1,0:T(8,128)(2,1)} %param.9) | copy-start | bytes 884740
  0.0 3.7 %collective-permute-start = (bf16[1,1,2,192,192]{4,3,2,1,0:T(8,128)(2,1)}, bf16[1,1,2,192,192]{4,3,2,1,0:T(8,128)(2,1)S(1)}, u32[]{:S(2)}, u32[]{:S(2)}) collective-permute-start(bf16[1,1,2,192,192]{4,3,2,1,0:T(8,128)(2,1)} %sigma.1), channel_id=1, source_target_pairs={{1,0},{2,1},{3,2},{4,3},{5,4},{6,5},{7,6},{0,7},{9,8},{10,9},{11,1... | collective-permute-start | bytes 442376 | tf_op jit(solution)/shard_map/ppermute | solution.py:162
  0.2 0.9 %copy-start.3 = (bf16[1,1,2,192,192]{4,3,2,1,0:T(8,128)(2,1)S(1)}, bf16[1,1,2,192,192]{4,3,2,1,0:T(8,128)(2,1)}, u32[]{:S(2)}) copy-start(bf16[1,1,2,192,192]{4,3,2,1,0:T(8,128)(2,1)} %green.1) | copy-start | bytes 442372
  1.1 0.9 %copy-start.4 = (bf16[1,1,2,192,192]{4,3,2,1,0:T(8,128)(2,1)S(1)}, bf16[1,1,2,192,192]{4,3,2,1,0:T(8,128)(2,1)}, u32[]{:S(2)}) copy-start(bf16[1,1,2,192,192]{4,3,2,1,0:T(8,128)(2,1)} %sigma.1) | copy-start | bytes 442372
  2.0 0.9 %copy-start.5 = (bf16[256,256]{1,0:T(8,128)(2,1)S(1)}, bf16[256,256]{1,0:T(8,128)(2,1)}, u32[]{:S(2)}) copy-start(bf16[256,256]{1,0:T(8,128)(2,1)} %constant.4.clone.forward) | copy-start | bytes 393220
  2.9 0.9 %copy-start.1 = (bf16[1,1,2,192,192]{4,3,2,1,0:T(8,128)(2,1)S(1)}, bf16[1,1,2,192,192]{4,3,2,1,0:T(8,128)(2,1)}, u32[]{:S(2)}) copy-start(bf16[1,1,2,192,192]{4,3,2,1,0:T(8,128)(2,1)} %coupling.1) | copy-start | bytes 442372

commit v5 on v4

--- a/solution.py
+++ b/solution.py
@@ -15,16 +15,16 @@
 FREQ = 128
 LANES = 128
 FIRST = [
-    10, 20, 12, 31, 50, 55, 19, 56, 43, 45, 0, 21, 1, 16, 8, 22,
-    11, 54, 53, 42, 24, 29, 18, 33, 30, 28, 49, 61, 44, 40, 17, 48,
-    38, 59, 62, 39, 14, 7, 36, 51, 46, 35, 47, 15, 57, 26, 27, 5,
-    2, 13, 32, 58, 37, 23, 6, 34, 52, 4, 3, 63, 25, 9, 60, 41,
+    43, 24, 28, 55, 34, 13, 18, 7, 40, 26, 50, 36, 59, 41, 1, 63,
+    52, 61, 47, 8, 3, 32, 58, 35, 16, 51, 56, 60, 54, 11, 12, 0,
+    15, 62, 9, 31, 33, 5, 14, 25, 49, 30, 19, 39, 21, 45, 17, 20,
+    22, 37, 10, 42, 38, 2, 57, 29, 44, 23, 4, 6, 46, 48, 27, 53,
 ]
 SECOND = [
-    10, 20, 12, 31, 50, 55, 19, 56, 43, 45, 0, 21, 1, 16, 8, 22,
-    11, 54, 53, 42, 24, 29, 18, 33, 30, 28, 49, 61, 44, 40, 17, 48,
-    38, 59, 62, 39, 14, 7, 36, 51, 46, 35, 47, 15, 57, 26, 27, 5,
-    2, 13, 32, 58, 37, 23, 6, 34, 52, 4, 3, 63, 25, 9, 60, 41,
+    41, 29, 52, 54, 27, 35, 25, 6, 30, 42, 56, 7, 40, 49, 53, 18,
+    36, 26, 0, 22, 62, 2, 43, 50, 12, 32, 37, 4, 48, 46, 58, 16,
+    38, 3, 39, 23, 1, 20, 51, 14, 8, 59, 34, 31, 5, 57, 45, 47,
+    21, 10, 61, 9, 11, 15, 17, 55, 33, 13, 19, 44, 60, 28, 63, 24,
 ]
 
 

time: 62.6 us -> 60.5 us (0.966)
  blocking collectives: 56.2 us -> 54.2 us
    all_to_all x1, blocking collectives: 32.1 us -> 29.2 us  [shards(): lax.all_to_all(lesser, 'energy', split_axis=0, concat_axis=0, axis_index_...]
    all_to_all x1, blocking collectives: 24.1 us -> 25 us  [shards(): lax.all_to_all(joined, 'energy', split_axis=0, concat_axis=0, axis_index_...]
where the time goes in v5:
time: 60.5 us; the launch traced here: 60.3 us
  blocking collectives  54.2 us (90%)
  Pallas kernels  2.98 us (5%)
  local copies, waits for them, and re-layouts  2.29 us (4%)
    all_to_all x1, blocking collectives, shards(): lax.all_to_all(lesser, 'energy', split_axis=0, concat_axis=0, axis_index_...  29.2 us
    all_to_all x1, blocking collectives, shards(): lax.all_to_all(joined, 'energy', split_axis=0, concat_axis=0, axis_index_...  25 us
    pallas_call x5, Pallas kernels, call(): pl.pallas_call(kernel, out_shape=shapes, in_specs=[vmem] * len(values), o...  2.98 us
    unnamed x12, local copies, waits for them, and re-layouts  2.29 us
  transfers between devices with their start and end apart: 1, of which 1 were waited for; matrix products, arithmetic and copies ran while one was open for 0% of the time, Pallas kernels for 1%

profile of v5, /device:TPU:24, one launch (start us, length us, event | category | flops | bytes accessed | tf_op | source)
XLA Modules:
  0.0 60.3 jit_solution(13556323123638013156)
XLA Ops:
  0.0 0.0 copy-start.2
  0.0 0.0 copy-start
  0.0 0.2 collective-permute-start
  0.2 0.0 copy-start.3
  0.2 0.9 %copy-done.3 = bf16[1,1,2,192,192]{4,3,2,1,0:T(8,128)(2,1)S(1)} copy-done((bf16[1,1,2,192,192]{4,3,2,1,0:T(8,128)(2,1)S(1)}, bf16[1,1,2,192,192]{4,3,2,1,0:T(8,128)(2,1)}, u32[]{:S(2)}) %copy-start.3) | copy-done | bytes 147480
  1.1 0.0 copy-start.4
  1.1 0.9 %copy-done.4 = bf16[1,1,2,192,192]{4,3,2,1,0:T(8,128)(2,1)S(1)} copy-done((bf16[1,1,2,192,192]{4,3,2,1,0:T(8,128)(2,1)S(1)}, bf16[1,1,2,192,192]{4,3,2,1,0:T(8,128)(2,1)}, u32[]{:S(2)}) %copy-start.4) | copy-done | bytes 147480
  2.0 0.0 copy-start.5
  2.0 0.6 %shard_map.64.own = f32[128,576]{1,0:T(8,128)S(1)} custom-call(bf16[1,1,2,192,192]{4,3,2,1,0:T(8,128)(2,1)S(1)} %copy-done.3, bf16[1,1,2,192,192]{4,3,2,1,0:T(8,128)(2,1)S(1)} %copy-done.4), custom_call_target="tpu_custom_call" | custom-call | flops 113246208 | bytes 600000 | tf_op jit(solution)/shard_map/pallas_call | solution.py:149
  2.7 0.0 copy-done.2
  2.7 0.0 copy-done
  2.7 0.2 copy-done.5
  2.9 0.0 copy-start.1
  2.9 0.1 shard_map.65
  3.1 0.6 collective-permute-done.sigma
  3.7 0.2 copy-done.1
  3.9 0.6 %shard_map.66 = bf16[64,2,576]{2,1,0:T(2,128)(2,1)S(1)} custom-call(bf16[1,1,2,192,192]{4,3,2,1,0:T(8,128)(2,1)S(1)} %copy-done.1, bf16[1,1,2,192,192]{4,3,2,1,0:T(8,128)(2,1)S(1)} %collective-permute-done.sigma, f32[128,576]{1,0:T(8,128)S(1)} %shard_map.64.own), custom_call_target="tpu_custom_call" | custom-call | flops 113246208 | bytes 700000 | tf_op jit(solution)/shard_map/pallas_call | solution.py:149
  4.5 29.2 %all_to_all.10.columns = bf16[64,2,576]{2,1,0:T(2,128)(2,1)S(1)} all-to-all(bf16[64,2,576]{2,1,0:T(2,128)(2,1)S(1)} %shard_map.66), channel_id=1, replica_groups={{344,192,224,440,272,104,144,56,320,208,400,288,472,328,8,504,416,488,3..., dimensions={0} | all-to-all | bytes 294912 | tf_op jit(solution)/shard_map/all_to_all | solution.py:174
  33.7 0.6 %shard_map.67 = bf16[64,2,576]{2,1,0:T(2,128)(2,1)S(1)} custom-call(bf16[64,2,576]{2,1,0:T(2,128)(2,1)S(1)} %all_to_all.10.columns, bf16[2,128,576]{2,1,0:T(8,128)(2,1)S(1)} %get-tuple-element.16.screened, bf16[256,256]{1,0:T(8,128)(2,1)S(1)} %get-tuple-element.17.forward, bf16[128,768]{1,0:T(8,128)(2,1)S(1)} %get-tuple-element.18.backward), custom_call_target="tpu_custom_call" | custom-call | flops 188743680 | bytes 800000 | tf_op jit(solution)/shard_map/pallas_call | solution.py:149
  34.4 25.0 %all_to_all.11.packed = bf16[64,2,576]{2,1,0:T(2,128)(2,1)S(1)} all-to-all(bf16[64,2,576]{2,1,0:T(2,128)(2,1)S(1)} %shard_map.67), channel_id=1, replica_groups={{328,232,416,432,216,280,200,48,240,336,448,56,320,392,424,144,288,208,..., dimensions={0} | all-to-all | bytes 294912 | tf_op jit(solution)/shard_map/all_to_all | solution.py:176
  59.4 0.9 %shard_map.68 = bf16[1,1,2,192,192]{4,3,2,1,0:T(8,128)(2,1)} custom-call(bf16[64,2,576]{2,1,0:T(2,128)(2,1)S(1)} %all_to_all.11.packed), custom_call_target="tpu_custom_call" | custom-call | flops 1000000 | bytes 300000 | tf_op jit(solution)/shard_map/pallas_call | solution.py:149
Async XLA Ops:
  0.0 2.7 %copy-start.2 = (bf16[128,768]{1,0:T(8,128)(2,1)S(1)}, bf16[128,768]{1,0:T(8,128)(2,1)}, u32[]{:S(2)}) copy-start(bf16[128,768]{1,0:T(8,128)(2,1)} %constant.5.clone.backward) | copy-start | bytes 589828
  0.0 2.7 %copy-start = (bf16[1,2,128,576]{2,3,1,0:T(8,128)(2,1)S(1)}, bf16[1,2,128,576]{2,3,1,0:T(8,128)(2,1)}, u32[]{:S(2)}) copy-start(bf16[1,2,128,576]{2,3,1,0:T(8,128)(2,1)} %param.9) | copy-start | bytes 884740
  0.0 3.7 %collective-permute-start = (bf16[1,1,2,192,192]{4,3,2,1,0:T(8,128)(2,1)}, bf16[1,1,2,192,192]{4,3,2,1,0:T(8,128)(2,1)S(1)}, u32[]{:S(2)}, u32[]{:S(2)}) collective-permute-start(bf16[1,1,2,192,192]{4,3,2,1,0:T(8,128)(2,1)} %sigma.1), channel_id=1, source_target_pairs={{1,0},{2,1},{3,2},{4,3},{5,4},{6,5},{7,6},{0,7},{9,8},{10,9},{11,1... | collective-permute-start | bytes 442376 | tf_op jit(solution)/shard_map/ppermute | solution.py:162
  0.2 0.9 %copy-start.3 = (bf16[1,1,2,192,192]{4,3,2,1,0:T(8,128)(2,1)S(1)}, bf16[1,1,2,192,192]{4,3,2,1,0:T(8,128)(2,1)}, u32[]{:S(2)}) copy-start(bf16[1,1,2,192,192]{4,3,2,1,0:T(8,128)(2,1)} %green.1) | copy-start | bytes 442372
  1.1 0.9 %copy-start.4 = (bf16[1,1,2,192,192]{4,3,2,1,0:T(8,128)(2,1)S(1)}, bf16[1,1,2,192,192]{4,3,2,1,0:T(8,128)(2,1)}, u32[]{:S(2)}) copy-start(bf16[1,1,2,192,192]{4,3,2,1,0:T(8,128)(2,1)} %sigma.1) | copy-start | bytes 442372
  2.0 0.9 %copy-start.5 = (bf16[256,256]{1,0:T(8,128)(2,1)S(1)}, bf16[256,256]{1,0:T(8,128)(2,1)}, u32[]{:S(2)}) copy-start(bf16[256,256]{1,0:T(8,128)(2,1)} %constant.4.clone.forward) | copy-start | bytes 393220
  2.9 0.9 %copy-start.1 = (bf16[1,1,2,192,192]{4,3,2,1,0:T(8,128)(2,1)S(1)}, bf16[1,1,2,192,192]{4,3,2,1,0:T(8,128)(2,1)}, u32[]{:S(2)}) copy-start(bf16[1,1,2,192,192]{4,3,2,1,0:T(8,128)(2,1)} %coupling.1) | copy-start | bytes 442372

commit v6 on v5

--- a/solution.py
+++ b/solution.py
@@ -15,16 +15,16 @@
 FREQ = 128
 LANES = 128
 FIRST = [
+    43, 15, 45, 21, 49, 13, 33, 47, 0, 22, 34, 40, 26, 14, 30, 17,
+    41, 55, 20, 52, 60, 2, 28, 5, 62, 8, 16, 19, 12, 56, 63, 54,
+    10, 37, 59, 24, 7, 53, 3, 11, 25, 46, 35, 39, 57, 36, 27, 32,
+    1, 51, 31, 38, 58, 6, 50, 61, 42, 23, 29, 9, 48, 44, 18, 4,
+]
+SECOND = [
     43, 24, 28, 55, 34, 13, 18, 7, 40, 26, 50, 36, 59, 41, 1, 63,
     52, 61, 47, 8, 3, 32, 58, 35, 16, 51, 56, 60, 54, 11, 12, 0,
     15, 62, 9, 31, 33, 5, 14, 25, 49, 30, 19, 39, 21, 45, 17, 20,
     22, 37, 10, 42, 38, 2, 57, 29, 44, 23, 4, 6, 46, 48, 27, 53,
-]
-SECOND = [
-    41, 29, 52, 54, 27, 35, 25, 6, 30, 42, 56, 7, 40, 49, 53, 18,
-    36, 26, 0, 22, 62, 2, 43, 50, 12, 32, 37, 4, 48, 46, 58, 16,
-    38, 3, 39, 23, 1, 20, 51, 14, 8, 59, 34, 31, 5, 57, 45, 47,
-    21, 10, 61, 9, 11, 15, 17, 55, 33, 13, 19, 44, 60, 28, 63, 24,
 ]
 
 
@@ -76,16 +76,17 @@
         out[place] = chunks[owner]
 
 
-def prepare_kernel(screened, forward, backward, turned, forward_out, backward_out):
+def prepare_kernel(screened, table, turned, table_out):
     for part in range(2):
         turned[part] = screened[0, part].T
-    forward_out[...] = forward[...]
-    backward_out[...] = backward[...]
-
-
-def convolve_kernel(columns, screened, forward, backward, out):
+    table_out[...] = table[...]
+
+
+def convolve_kernel(columns, screened, table, out):
     value = columns[...].reshape(2 * OWNERS, WIDTH)
-    spectrum = dot(forward[...], jnp.concatenate([value, value], axis=0))
+    forward = table[:, : 4 * OWNERS]
+    backward = jnp.concatenate([table[:FREQ, 4 * OWNERS :], table[FREQ:, 4 * OWNERS :]], axis=1)
+    spectrum = dot(forward, jnp.concatenate([value, value], axis=0))
     spec_real, spec_imag = spectrum[:FREQ], spectrum[FREQ:]
     screen_real = screened[0].astype(jnp.float32)
     screen_imag = screened[1].astype(jnp.float32)
@@ -94,7 +95,7 @@
     conv = jnp.concatenate([conv_real, conv_imag], axis=0)
     high = conv.astype(jnp.bfloat16)
     low = (conv - high.astype(jnp.float32)).astype(jnp.bfloat16)
-    out[...] = dot(backward[...], jnp.concatenate([high, high, low], axis=0)).astype(jnp.bfloat16).reshape(out.shape)
+    out[...] = dot(backward, jnp.concatenate([high, high, low], axis=0)).astype(jnp.bfloat16).reshape(out.shape)
 
 
 def unpack_kernel(packed, out, flat, rows, near, sems):
@@ -134,10 +135,9 @@
     backward = np.stack([to_real, to_imag], axis=1)[SECOND].reshape(2 * OWNERS, 2 * FREQ) / FREQ
     forward_high, forward_low = split(forward)
     back_high, back_low = split(backward)
-    return (
-        np.concatenate([forward_high, forward_low], axis=1),
-        np.concatenate([back_high, back_low, back_high], axis=1),
-    )
+    backward = np.concatenate([back_high, back_low, back_high], axis=1)
+    halves = np.split(backward, 2, axis=1)
+    return np.concatenate([forward_high, forward_low, np.concatenate(halves, axis=0)], axis=1)
 
 
 def shaped(shape, dtype=jnp.bfloat16):
@@ -164,15 +164,14 @@
     packed = shaped((OWNERS, 2, WIDTH))
     flops = 16 * M**3
     (own,) = call(own_kernel, [shaped((2 * OWNERS, WIDTH), jnp.float32)], flops, 600000, green_block, sigma_lesser, scratch=planes)
-    forward, backward = tables()
-    turned, forward, backward = call(
-        prepare_kernel, [shaped((2, FREQ, WIDTH)), shaped(forward.shape), shaped(backward.shape)], flops, 1200000,
-        screened.transpose(0, 1, 3, 2), jnp.asarray(forward), jnp.asarray(backward),
-    )
-    own, turned, forward, backward = lax.optimization_barrier((own, turned, forward, backward))
+    table = jnp.asarray(tables())
+    turned, table = call(
+        prepare_kernel, [shaped((2, FREQ, WIDTH)), shaped(table.shape)], flops, 1200000, screened.transpose(0, 1, 3, 2), table
+    )
+    own, turned, table = lax.optimization_barrier((own, turned, table))
     (lesser,) = call(next_kernel, [packed], flops, 700000, coupling, sigma_next, own, scratch=planes)
     columns = lax.all_to_all(lesser, "energy", split_axis=0, concat_axis=0, axis_index_groups=[FIRST], tiled=True)
-    (joined,) = call(convolve_kernel, [packed], 2 * 5 * 256 * 128 * WIDTH, 800000, columns, turned, forward, backward)
+    (joined,) = call(convolve_kernel, [packed], 2 * 5 * 256 * 128 * WIDTH, 800000, columns, turned, table)
     returned = lax.all_to_all(joined, "energy", split_axis=0, concat_axis=0, axis_index_groups=[SECOND], tiled=True)
     (result,) = call(
         unpack_kernel, [shaped(sigma_lesser.shape)], 1000000, 300000, returned,

time: 60.5 us -> 60.4 us (level)
    unnamed x12 -> x10, local copies, waits for them, and re-layouts: 2.29 us -> 1.87 us
where the time goes in v6:
time: 60.4 us; the launch traced here: 60.2 us
  blocking collectives  54.3 us (90%)
  Pallas kernels  2.97 us (5%)
  local copies, waits for them, and re-layouts  1.87 us (3%)
  waiting for transfers between devices  0.83 us (1%)
    all_to_all x1, blocking collectives, shards(): lax.all_to_all(lesser, 'energy', split_axis=0, concat_axis=0, axis_index_...  29.8 us
    all_to_all x1, blocking collectives, shards(): lax.all_to_all(joined, 'energy', split_axis=0, concat_axis=0, axis_index_...  24.5 us
    pallas_call x5, Pallas kernels, call(): pl.pallas_call(kernel, out_shape=shapes, in_specs=[vmem] * len(values), o...  2.97 us
    unnamed x10, local copies, waits for them, and re-layouts  1.87 us
  transfers between devices with their start and end apart: 1, of which 1 were waited for; matrix products, arithmetic and copies ran while one was open for 0% of the time, Pallas kernels for 1%

profile of v6, /device:TPU:24, one launch (start us, length us, event | category | flops | bytes accessed | tf_op | source)
XLA Modules:
  0.0 60.2 jit_solution(4992924673975401719)
XLA Ops:
  0.0 0.0 copy-start
  0.0 0.0 copy-start.1
  0.0 0.2 collective-permute-start
  0.2 0.0 copy-start.3
  0.2 0.9 %copy-done.3 = bf16[1,1,2,192,192]{4,3,2,1,0:T(8,128)(2,1)S(1)} copy-done((bf16[1,1,2,192,192]{4,3,2,1,0:T(8,128)(2,1)S(1)}, bf16[1,1,2,192,192]{4,3,2,1,0:T(8,128)(2,1)}, u32[]{:S(2)}) %copy-start.3) | copy-done | bytes 147480
  1.1 0.0 copy-start.4
  1.1 0.9 %copy-done.4 = bf16[1,1,2,192,192]{4,3,2,1,0:T(8,128)(2,1)S(1)} copy-done((bf16[1,1,2,192,192]{4,3,2,1,0:T(8,128)(2,1)S(1)}, bf16[1,1,2,192,192]{4,3,2,1,0:T(8,128)(2,1)}, u32[]{:S(2)}) %copy-start.4) | copy-done | bytes 147480
  2.0 0.6 %shard_map.55.own = f32[128,576]{1,0:T(8,128)S(1)} custom-call(bf16[1,1,2,192,192]{4,3,2,1,0:T(8,128)(2,1)S(1)} %copy-done.3, bf16[1,1,2,192,192]{4,3,2,1,0:T(8,128)(2,1)S(1)} %copy-done.4), custom_call_target="tpu_custom_call" | custom-call | flops 113246208 | bytes 600000 | tf_op jit(solution)/shard_map/pallas_call | solution.py:149
  2.7 0.0 copy-done
  2.7 0.0 copy-done.1
  2.7 0.0 copy-start.2
  2.7 0.1 shard_map.56
  2.9 0.8 %collective-permute-done.sigma = bf16[1,1,2,192,192]{4,3,2,1,0:T(8,128)(2,1)S(1)} collective-permute-done((bf16[1,1,2,192,192]{4,3,2,1,0:T(8,128)(2,1)}, bf16[1,1,2,192,192]{4,3,2,1,0:T(8,128)(2,1)S(1)}, u32[]{:S(2)}, u32[]{:S(2)}) %collective-permute-start) | collective-permute-done | bytes 147488 | tf_op jit(solution)/shard_map/ppermute | solution.py:162
  3.7 0.0 copy-done.2
  3.7 0.6 %shard_map.57 = bf16[64,2,576]{2,1,0:T(2,128)(2,1)S(1)} custom-call(bf16[1,1,2,192,192]{4,3,2,1,0:T(8,128)(2,1)S(1)} %copy-done.2, bf16[1,1,2,192,192]{4,3,2,1,0:T(8,128)(2,1)S(1)} %collective-permute-done.sigma, f32[128,576]{1,0:T(8,128)S(1)} %shard_map.55.own), custom_call_target="tpu_custom_call" | custom-call | flops 113246208 | bytes 700000 | tf_op jit(solution)/shard_map/pallas_call | solution.py:149
  4.3 29.8 %all_to_all.10.columns = bf16[64,2,576]{2,1,0:T(2,128)(2,1)S(1)} all-to-all(bf16[64,2,576]{2,1,0:T(2,128)(2,1)S(1)} %shard_map.57), channel_id=1, replica_groups={{344,120,360,168,392,104,264,376,0,176,272,320,208,112,240,136,328,440,..., dimensions={0} | all-to-all | bytes 294912 | tf_op jit(solution)/shard_map/all_to_all | solution.py:173
  34.1 0.6 %shard_map.58 = bf16[64,2,576]{2,1,0:T(2,128)(2,1)S(1)} custom-call(bf16[64,2,576]{2,1,0:T(2,128)(2,1)S(1)} %all_to_all.10.columns, bf16[2,128,576]{2,1,0:T(8,128)(2,1)S(1)} %get-tuple-element.13.screened, bf16[256,640]{1,0:T(8,128)(2,1)S(1)} %get-tuple-element.14.table), custom_call_target="tpu_custom_call" | custom-call | flops 188743680 | bytes 800000 | tf_op jit(solution)/shard_map/pallas_call | solution.py:149
  34.8 24.5 %all_to_all.11.packed = bf16[64,2,576]{2,1,0:T(2,128)(2,1)S(1)} all-to-all(bf16[64,2,576]{2,1,0:T(2,128)(2,1)S(1)} %shard_map.58), channel_id=1, replica_groups={{344,192,224,440,272,104,144,56,320,208,400,288,472,328,8,504,416,488,3..., dimensions={0} | all-to-all | bytes 294912 | tf_op jit(solution)/shard_map/all_to_all | solution.py:175
  59.3 0.9 %shard_map.59 = bf16[1,1,2,192,192]{4,3,2,1,0:T(8,128)(2,1)} custom-call(bf16[64,2,576]{2,1,0:T(2,128)(2,1)S(1)} %all_to_all.11.packed), custom_call_target="tpu_custom_call" | custom-call | flops 1000000 | bytes 300000 | tf_op jit(solution)/shard_map/pallas_call | solution.py:149
Async XLA Ops:
  0.0 2.7 %copy-start = (bf16[256,640]{1,0:T(8,128)(2,1)S(1)}, bf16[256,640]{1,0:T(8,128)(2,1)}, u32[]{:S(2)}) copy-start(bf16[256,640]{1,0:T(8,128)(2,1)} %constant.2.clone.table) | copy-start | bytes 983044
  0.0 2.7 %copy-start.1 = (bf16[1,2,128,576]{2,3,1,0:T(8,128)(2,1)S(1)}, bf16[1,2,128,576]{2,3,1,0:T(8,128)(2,1)}, u32[]{:S(2)}) copy-start(bf16[1,2,128,576]{2,3,1,0:T(8,128)(2,1)} %param.8) | copy-start | bytes 884740
  0.0 3.7 %collective-permute-start = (bf16[1,1,2,192,192]{4,3,2,1,0:T(8,128)(2,1)}, bf16[1,1,2,192,192]{4,3,2,1,0:T(8,128)(2,1)S(1)}, u32[]{:S(2)}, u32[]{:S(2)}) collective-permute-start(bf16[1,1,2,192,192]{4,3,2,1,0:T(8,128)(2,1)} %sigma.1), channel_id=1, source_target_pairs={{1,0},{2,1},{3,2},{4,3},{5,4},{6,5},{7,6},{0,7},{9,8},{10,9},{11,1... | collective-permute-start | bytes 442376 | tf_op jit(solution)/shard_map/ppermute | solution.py:162
  0.2 0.9 %copy-start.3 = (bf16[1,1,2,192,192]{4,3,2,1,0:T(8,128)(2,1)S(1)}, bf16[1,1,2,192,192]{4,3,2,1,0:T(8,128)(2,1)}, u32[]{:S(2)}) copy-start(bf16[1,1,2,192,192]{4,3,2,1,0:T(8,128)(2,1)} %green.1) | copy-start | bytes 442372
  1.1 0.9 %copy-start.4 = (bf16[1,1,2,192,192]{4,3,2,1,0:T(8,128)(2,1)S(1)}, bf16[1,1,2,192,192]{4,3,2,1,0:T(8,128)(2,1)}, u32[]{:S(2)}) copy-start(bf16[1,1,2,192,192]{4,3,2,1,0:T(8,128)(2,1)} %sigma.1) | copy-start | bytes 442372
  2.7 1.0 %copy-start.2 = (bf16[1,1,2,192,192]{4,3,2,1,0:T(8,128)(2,1)S(1)}, bf16[1,1,2,192,192]{4,3,2,1,0:T(8,128)(2,1)}, u32[]{:S(2)}) copy-start(bf16[1,1,2,192,192]{4,3,2,1,0:T(8,128)(2,1)} %coupling.1) | copy-start | bytes 442372
